TPU v7x, 128 devices: a whole 4x4x4 slice. The times are simulated.
128 devices in a mesh: dp: 16 (over z_hi, x, core), fsdp: 8 (over y, z_lo).
Axes of the slice: x: 4, y: 4, z: 4 (z_hi: 2, z_lo: 2; z = z_hi * 2 + z_lo), core: 2. Of those that a mesh axis runs over, the one named last changes fastest.
Arguments:
- layer_input: bfloat16 [65536, 8192], P(('dp', 'fsdp')), may hold values from -400 to 400
- rotated_grad: bfloat16 [65536, 512], P(('dp', 'fsdp')), may hold values from -24 to 24
- norm_gain: bfloat16 [8192], replicated, may hold values from 0.099609375 to 1.8984375
- key_weight: bfloat16 [8192, 512], P('fsdp'), may hold values from -3 to 3
- block_length: int32 [8, 16, 16], P('fsdp'), may hold values from 1 to 64, as said below
- block_owner: int32 [8, 16, 16], P('fsdp'), may hold values from 0 to 15, as said below
- block_source_offset: int32 [8, 16, 16], P('fsdp'), may hold values from 0 to 511, as said below
- block_pack_offset: int32 [8, 16, 16], P('fsdp'), may hold values from 0 to 511, as said below
- block_position: int32 [8, 16, 16], P('fsdp'), may hold values from 0 to 8128
Outputs:
- input_grad: bfloat16 [65536, 8192], P(('dp', 'fsdp'))
- weight_grad: float32 [8192, 512], P(('dp', 'fsdp'))
Inputs may be any that keep to these rules, and one draw needn't show every extreme that they name: `block_length`: in each column every loader shard holds 16 blocks that tile its 512 rows, one block for each pack owner; every owner receives one block from each loader shard of its column, and these tile its 512 rows. Every loader shard has one block of exactly 64 rows, and every owner receives one such block. `block_owner`: for each loader shard, the owners of its blocks are all different. `block_source_offset`: running sums of the lengths of a loader shard's blocks, in block order. `block_pack_offset`: blocks arriving at one owner do not intersect.
All inputs are finite; a program needn't handle non-finite values.
Results may differ from a plain program's by a relative error of at most 0.014.
Values may be sent and summed in bfloat16 or wider, within the bound.
No kernel may reach another device: no remote copies, remote signals or barrier semaphores. Data moves between devices by JAX's collectives and lax.ppermute only.
A program may use at most 128 MiB of HBM per device.

v0:
```python
import math

import jax
import jax.numpy as jnp
from jax import lax
from jax.sharding import PartitionSpec as P

HEAD = 128
KV_HEADS = 4


rope_base = 500000.0
norm_eps = 1e-05


def rope_back(rotated, position):
    half_head = HEAD // 2
    exponent = jnp.arange(half_head, dtype=jnp.float32) * (2.0 / HEAD)
    inverse = jnp.power(jnp.float32(rope_base), -exponent)
    angle = position.astype(jnp.float32)[:, None] * inverse[None, :]
    cosine = jnp.cos(angle)[:, None, :]
    sine = jnp.sin(angle)[:, None, :]
    grads = rotated.astype(jnp.float32).reshape(-1, KV_HEADS, HEAD)
    first_half = grads[..., :half_head]
    second_half = grads[..., half_head:]
    joined = jnp.concatenate(
        [first_half * cosine + second_half * sine, second_half * cosine - first_half * sine],
        axis=-1,
    )
    return joined.reshape(-1, KV_HEADS * HEAD).astype(jnp.bfloat16)


def body(
    layer_input,
    rotated_grad,
    norm_gain,
    key_weight,
    block_length,
    block_owner,
    block_source_offset,
    block_pack_offset,
    block_position,
):
    tok_rows, width = layer_input.shape
    loaders = lax.axis_size("dp")
    columns = lax.axis_size("fsdp")
    own_index = lax.axis_index("dp")
    capacity = 2 * tok_rows // loaders
    lengths = block_length[0]
    owners = block_owner[0]
    source_offsets = block_source_offset[0]
    pack_offsets = block_pack_offset[0]
    positions = block_position[0]
    shard_ids = jnp.arange(loaders, dtype=jnp.int32)
    slot_ids = jnp.arange(capacity, dtype=jnp.int32)
    own_lengths = lax.dynamic_index_in_dim(lengths, own_index, 0, keepdims=False)
    own_owners = lax.dynamic_index_in_dim(owners, own_index, 0, keepdims=False)
    own_offsets = lax.dynamic_index_in_dim(source_offsets, own_index, 0, keepdims=False)
    chosen = (own_owners[None, :] == shard_ids[:, None]).astype(jnp.int32)
    send_start = jnp.sum(chosen * own_offsets[None, :], axis=1)
    send_length = jnp.sum(chosen * own_lengths[None, :], axis=1)
    live = slot_ids[None, :] < send_length[:, None]
    send_rows = jnp.where(live, send_start[:, None] + slot_ids[None, :], 0)
    outgoing = jnp.take(layer_input, send_rows.reshape(-1), axis=0).reshape(
        loaders, capacity, width
    )
    outgoing = jnp.where(live[:, :, None], outgoing, jnp.zeros((), jnp.bfloat16))
    arrived = lax.all_to_all(outgoing, "dp", split_axis=0, concat_axis=0, tiled=True)
    mine = (owners == own_index).astype(jnp.int32)
    arrive_start = jnp.sum(mine * pack_offsets, axis=1)
    arrive_length = jnp.sum(mine * lengths, axis=1)
    arrive_position = jnp.sum(mine * positions, axis=1)
    packed_ids = jnp.arange(tok_rows, dtype=jnp.int32)
    lower = packed_ids[:, None] >= arrive_start[None, :]
    upper = packed_ids[:, None] < (arrive_start + arrive_length)[None, :]
    inside = (lower & upper).astype(jnp.int32)
    source = jnp.sum(inside * shard_ids[None, :], axis=1)
    first = jnp.sum(inside * arrive_start[None, :], axis=1)
    base_position = jnp.sum(inside * arrive_position[None, :], axis=1)
    offset_in = packed_ids - first
    position = base_position + offset_in
    packed = jnp.take(
        arrived.reshape(loaders * capacity, width), source * capacity + offset_in, axis=0
    )
    values = packed.astype(jnp.float32)
    inv_rms = lax.rsqrt(jnp.mean(values * values, axis=-1, keepdims=True) + norm_eps)
    gain = norm_gain.astype(jnp.float32)[None, :]
    normed = (values * inv_rms * gain).astype(jnp.bfloat16)
    key_grad = rope_back(rotated_grad, position)
    input_delta = lax.dot_general(
        key_grad,
        lax.all_gather(key_weight, "fsdp", axis=0, tiled=True),
        (((1,), (1,)), ((), ())),
        preferred_element_type=jnp.float32,
    )
    scaled = input_delta * gain
    inner = jnp.mean(scaled * values, axis=-1, keepdims=True)
    input_grad = (inv_rms * (scaled - values * inv_rms * inv_rms * inner)).astype(jnp.bfloat16)
    scale = 1.0 / math.sqrt(tok_rows * loaders * columns)
    weight_grad = lax.psum_scatter(
        lax.optimization_barrier(
            (
                lax.dot_general(
                    normed, key_grad, (((0,), (0,)), ((), ())), preferred_element_type=jnp.float32
                )
                * scale
            ).astype(jnp.bfloat16)
        ).astype(jnp.float32),
        ("dp", "fsdp"),
        scatter_dimension=0,
        tiled=True,
    )
    return (input_grad, weight_grad)


def solution(mesh):
    return jax.shard_map(
        body,
        mesh=mesh,
        in_specs=(
            P(("dp", "fsdp"), None),
            P(("dp", "fsdp"), None),
            P(),
            P("fsdp", None),
            P("fsdp", None, None),
            P("fsdp", None, None),
            P("fsdp", None, None),
            P("fsdp", None, None),
            P("fsdp", None, None),
        ),
        out_specs=(P(("dp", "fsdp"), None), P(("dp", "fsdp"), None)),
        check_vma=False,
    )
```

profile of v0, /device:TPU:1, one launch (start us, length us, event | category | flops | bytes accessed | tf_op | source)
XLA Modules:
  0.0 1100.7 jit_solution(615874684392385759)
XLA Ops:
  7.2 0.7 copy-done
  7.9 0.7 fusion.18
  8.6 0.1 select_reduce_fusion.5
  8.7 0.1 add_select_fusion
  8.8 0.1 iota_compare_fusion.3
  8.9 0.1 select_n.74
  9.0 32.4 %gather_fusion = bf16[1024,8192]{1,0:T(8,128)(2,1)} fusion(bf16[512,8192]{1,0:T(8,128)(2,1)} %param.9, s32[1024]{0:T(1024)S(1)} %broadcast_clamp_fusion), kind=kCustom, calls=%fused_computation | custom fusion | bytes 33558528 | tf_op jit(solution)/shard_map/jit(_take)/gather | solution.py:64
  41.3 14.3 %select_select_fusion = bf16[16,64,8192]{2,1,0:T(8,128)(2,1)} fusion(bf16[16,64,8192]{2,1,0:T(8,128)(2,1)} %bitcast.21, pred[16,64]{1,0:T(8,128)(4,1)S(1)} %get-tuple-element.17, pred[16,64]{1,0:T(8,128)(4,1)S(1)} %get-tuple-element.16), kind=kLoop, calls=%fused_computation.15 | loop fusion | flops 16777216 | bytes 33556480 | tf_op jit(solution)/shard_map/jit(_where)/select_n | solution.py:67
  55.7 9.3 all-to-all-start
  65.0 0.7 all-gather.2.cloned.1.call-update
  65.7 0.3 reshape.248
  66.1 0.1 select_reduce_fusion.6
  66.3 0.1 select_reduce_fusion.2
  66.4 1.0 multiply_cosine_fusion
  67.4 0.9 add_convert_fusion
  68.3 0.7 pad_maximum_fusion
  69.0 273.1 %all-to-all-done = bf16[16,64,8192]{2,1,0:T(8,128)(2,1)} async-done(((bf16[16,64,8192]{2,1,0:T(8,128)(2,1)}), bf16[16,64,8192]{2,1,0:T(8,128)(2,1)}, u32[]{:S(2)}, u32[]{:S(2)}) %all-to-all-start) | async-done | bytes 16777248 | tf_op jit(solution)/shard_map/all_to_all | solution.py:68
  342.2 23.7 %gather_fusion.1 = bf16[512,8192]{1,0:T(8,128)(2,1)} fusion(bf16[1024,8192]{1,0:T(8,128)(2,1)} %bitcast.5, s32[1024]{0:T(1024)S(1)} %pad_clamp_fusion), kind=kCustom, calls=%fused_computation.1 | custom fusion | bytes 16779264 | tf_op jit(solution)/shard_map/jit(_take)/gather | solution.py:82
  365.9 38.8 %all-gather.2.cloned.1.call-done = bf16[8192,512]{1,0:T(8,128)(2,1)} async-done(((bf16[1024,512]{1,0:T(8,128)(2,1)}), bf16[8192,512]{1,0:T(8,128)(2,1)}) %all-gather.2.cloned.1.call-update) | async-done | bytes 8388624 | tf_op jit(solution)/shard_map/all_gather | solution.py:92
  404.7 13.4 %fusion.7 = (f32[512]{0:T(512)S(1)}, f32[512]{0:T(512)S(1)}, f32[512,8192]{1,0:T(8,128)}) fusion(bf16[512,8192]{1,0:T(8,128)(2,1)} %gather_fusion.1, pred[512]{0:T(512)(128)(4,1)S(1)} %compare_and_fusion.1, f32[8192]{0:T(1024)S(1)} %convert_element_type.36, bf16[8192,512]{1,0:T(8,128)(2,1)} %all-gather.2.cloned.1.call-done, ...), kind=kOutput, calls=%fused_computation.12 | convolution fusion | flops 4324326400 | bytes 34116096 | tf_op jit(solution)/shard_map/dot_general | solution.py:90
  418.1 8.2 multiply_convert_fusion
  426.3 11.5 %convert_element_type.40 = f32[8192,512]{1,0:T(8,128)} convert(bf16[8192,512]{1,0:T(8,128)(2,1)} %multiply_convert_fusion) | non-fusion elementwise | flops 4194304 | bytes 25165824 | tf_op jit(solution)/shard_map/convert_element_type | solution.py:108
  437.9 13.4 %fusion.5 = bf16[512,8192]{1,0:T(8,128)(2,1)} fusion(f32[512,8192]{1,0:T(8,128)} %get-tuple-element.18, f32[512]{0:T(512)S(1)} %broadcast_multiply_fusion, f32[8192]{0:T(1024)S(1)} %convert_element_type.36, f32[512]{0:T(512)S(1)} %add_rsqrt_fusion, bf16[512,8192]{1,0:T(8,128)(2,1)} %gather_fusion.1, pred[512]{0:T(512)(128)(4,1)S(1)} %compare_and_fusion.1), kind=kLoop, calls=%fused_computation.10 | loop fusion | flops 37748736 | bytes 33591808 | tf_op jit(solution)/shard_map/convert_element_type | solution.py:98
  451.2 642.6 %reduce-scatter.2.cloned.1.call-done = f32[64,512]{1,0:T(8,128)} async-done(((f32[8192,512]{1,0:T(8,128)}), f32[64,512]{1,0:T(8,128)}) %reduce-scatter.2.cloned.1.call-update) | async-done | bytes 131088 | tf_op jit(solution)/shard_map/reduce_scatter | solution.py:100
  (32 shorter events, 0.2 us)
Async XLA Ops:
  7.2 0.7 copy-start
  55.6 10.1 copy-start.4
  55.6 10.1 copy-start.3
  55.6 10.5 copy-start.5
  55.6 10.5 copy-start.6
  55.6 10.5 copy-start.7
  55.7 10.5 copy-start.8
  55.7 286.5 %all-to-all-start = ((bf16[16,64,8192]{2,1,0:T(8,128)(2,1)}), bf16[16,64,8192]{2,1,0:T(8,128)(2,1)}, u32[]{:S(2)}, u32[]{:S(2)}) async-start(bf16[16,64,8192]{2,1,0:T(8,128)(2,1)} %select_select_fusion), calls=%async_computation | async-start | bytes 33554432 | tf_op jit(solution)/shard_map/all_to_all | solution.py:68
  64.9 339.7 %all-gather.2.cloned.1.call-start = ((), (), s32[]{:S(2)}) async-start(), calls=%async_computation.2 | async-start | bytes 9437184 | tf_op jit(solution)/shard_map/all_gather | solution.py:92
  65.7 1028.2 %reduce-scatter.2.cloned.1.call-start = ((), (), s32[]{:S(2)}) async-start(), calls=%async_computation.3 | async-start | bytes 16908288 | tf_op jit(solution)/shard_map/reduce_scatter | solution.py:100
  404.7 13.4 %copy-start.2 = (bf16[512,8192]{1,0:T(8,128)(2,1)S(1)}, bf16[512,8192]{1,0:T(8,128)(2,1)}, u32[]{:S(2)}) copy-start(bf16[512,8192]{1,0:T(8,128)(2,1)} %gather_fusion.1) | copy-start | bytes 25165828
  437.8 656.0 %copy-start.1 = (s32[1,16,16]{2,1,0:T(8,128)S(1)}, s32[1,16,16]{2,1,0:T(8,128)}, u32[]{:S(2)}) copy-start(s32[1,16,16]{2,1,0:T(8,128)} %param.15) | copy-start | bytes 3076
Sparse Core Ops, SparseCore 0:
  67.4 337.2 all-gather.1
  438.0 655.8 reduce-scatter.1
where the time goes:
time: 1120 us; the launch traced here: 1100 us
  waiting for transfers between devices  955 us (85%)
  local copies, waits for them, and re-layouts  57.9 us (5%)
  other arithmetic  42.3 us (4%)
  matrix products  21.6 us (2%)
  between operations  14.2 us (1%)
    reduce_scatter x1, waiting for transfers between devices, body(): lax.psum_scatter(lax.optimization_barrier((lax.dot_general(normed, key_gr...  643 us
    all_to_all x1, waiting for transfers between devices, body(): lax.all_to_all(outgoing, 'dp', split_axis=0, concat_axis=0, tiled=True)  273 us
    all_gather x1, waiting for transfers between devices, body(): lax.all_gather(key_weight, 'fsdp', axis=0, tiled=True)  38.8 us
    gather x1, local copies, waits for them, and re-layouts, body(): jnp.take(layer_input, send_rows.reshape(-1), axis=0)  32.4 us
    gather x1, local copies, waits for them, and re-layouts, body(): jnp.take(arrived.reshape(loaders * capacity, width), source * capacity +...  23.7 us
  transfers between devices with their start and end apart: 3, of which 3 were waited for; matrix products, arithmetic and copies ran while one was open for 4% of the time, Pallas kernels for 0%

commit v1 on v0

v1 whole, which is shorter than its diff:
```python
import math

import jax
import jax.numpy as jnp
from jax import lax
from jax.sharding import PartitionSpec as P

HEAD = 128
KV_HEADS = 4
AXES = ("dp", "fsdp")

rope_base = 500000.0
norm_eps = 1e-05


def place(zh, x, c, y, zl):
    return ((((zh % 2) * 4 + x % 4) * 2 + c % 2) * 4 + y % 4) * 2 + zl % 2


def perm(step):
    pairs = []
    for zh in range(2):
        for x in range(4):
            for c in range(2):
                for y in range(4):
                    for zl in range(2):
                        pairs.append((place(zh, x, c, y, zl), place(*step(zh, x, c, y, zl))))
    return pairs


def along_core(v):
    return lax.ppermute(v, AXES, perm(lambda zh, x, c, y, zl: (zh, x, c + 1, y, zl)))


def along_x(v, n):
    return lax.ppermute(v, AXES, perm(lambda zh, x, c, y, zl: (zh, x + n, c, y, zl)))


def along_y(v, n):
    return lax.ppermute(v, AXES, perm(lambda zh, x, c, y, zl: (zh, x, c, y + n, zl)))


def along_z(v, n):
    def step(zh, x, c, y, zl):
        z = (zh * 2 + zl + n) % 4
        return (z // 2, x, c, y, z % 2)

    return lax.ppermute(v, AXES, perm(step))


def swap_zlo(v):
    return lax.ppermute(v, AXES, perm(lambda zh, x, c, y, zl: (zh, x, c, y, zl + 1)))


def pick(v, i, axis=0):
    return lax.dynamic_index_in_dim(v, i, axis, keepdims=False)


def rope_back(rotated, position):
    half_head = HEAD // 2
    exponent = jnp.arange(half_head, dtype=jnp.float32) * (2.0 / HEAD)
    inverse = jnp.power(jnp.float32(rope_base), -exponent)
    angle = position.astype(jnp.float32)[:, None] * inverse[None, :]
    cosine = jnp.cos(angle)
    sine = jnp.sin(angle)
    cos_full = jnp.concatenate([cosine, cosine] * KV_HEADS, axis=1)
    sin_full = jnp.concatenate([sine, -sine] * KV_HEADS, axis=1)
    grads = rotated.astype(jnp.float32)
    halves = [grads[:, i * half_head : (i + 1) * half_head] for i in range(2 * KV_HEADS)]
    swapped = jnp.concatenate([halves[i ^ 1] for i in range(2 * KV_HEADS)], axis=1)
    return (grads * cos_full + swapped * sin_full).astype(jnp.bfloat16)


def body(
    layer_input,
    rotated_grad,
    norm_gain,
    key_weight,
    block_length,
    block_owner,
    block_source_offset,
    block_pack_offset,
    block_position,
):
    tok_rows, width = layer_input.shape
    kv = rotated_grad.shape[1]
    loaders = lax.axis_size("dp")
    columns = lax.axis_size("fsdp")
    dp = lax.axis_index("dp")
    fs = lax.axis_index("fsdp")
    zh, xx, core = dp // 8, (dp // 2) % 4, dp % 2
    yy, zl = fs // 2, fs % 2
    zz = zh * 2 + zl
    capacity = 2 * tok_rows // loaders
    lengths = block_length[0]
    owners = block_owner[0]
    source_offsets = block_source_offset[0]
    pack_offsets = block_pack_offset[0]
    positions = block_position[0]
    shard_ids = jnp.arange(loaders, dtype=jnp.int32)
    slot_ids = jnp.arange(capacity, dtype=jnp.int32)
    row_ids = jnp.arange(tok_rows, dtype=jnp.int32)

    mine = (owners == dp).astype(jnp.int32)
    arrive_start = jnp.sum(mine * pack_offsets, axis=1)
    arrive_length = jnp.sum(mine * lengths, axis=1)
    arrive_position = jnp.sum(mine * positions, axis=1)
    inside = (
        (row_ids[:, None] >= arrive_start[None, :])
        & (row_ids[:, None] < (arrive_start + arrive_length)[None, :])
    ).astype(jnp.int32)
    position = row_ids + jnp.sum(inside * (arrive_position - arrive_start)[None, :], axis=1)

    chosen = (pick(owners, dp)[None, :] == shard_ids[:, None]).astype(jnp.int32)
    send_start = jnp.sum(chosen * pick(source_offsets, dp)[None, :], axis=1)
    send_length = jnp.sum(chosen * pick(lengths, dp)[None, :], axis=1)

    def spread(start, length):
        row = jnp.where(slot_ids[None, :] < length[:, None], start[:, None] + slot_ids[None, :], -1)
        return (row.reshape(-1)[:, None] == row_ids[None, :]).astype(jnp.bfloat16)

    to_owner = spread(send_start, send_length)
    to_loader = spread(arrive_start, arrive_length)

    def move(matrix, rows):
        return jnp.dot(matrix, rows, preferred_element_type=jnp.float32).astype(jnp.bfloat16)

    def place_rows(matrix, rows):
        return lax.dot_general(
            matrix, rows, (((0,), (0,)), ((), ())), preferred_element_type=jnp.float32
        ).astype(jnp.bfloat16)

    def exchange(rows):
        blocks = rows.reshape(loaders, capacity, rows.shape[1])
        return lax.all_to_all(blocks, "dp", split_axis=0, concat_axis=0, tiled=True).reshape(rows.shape)

    key_grad = rope_back(rotated_grad, position)
    key_back = exchange(move(to_loader, key_grad))
    arrived = exchange(move(to_owner, layer_input))
    key_loader = place_rows(to_owner, key_back)

    depth = key_weight.shape[0] // 2
    half = pick(key_weight.reshape(2, depth, kv), core)
    other = swap_zlo(half)
    pair = jnp.where(zl == 0, jnp.stack([half, other]), jnp.stack([other, half]))
    whole = jnp.zeros((4, 2, depth, kv), jnp.bfloat16)
    whole = lax.dynamic_update_index_in_dim(whole, pair, yy, 0)
    for n in (1, 3, 2):
        whole = lax.dynamic_update_index_in_dim(whole, along_y(pair, n), (yy - n) % 4, 0)
    swapped = along_core(whole)
    weight = jnp.where(core == 0, jnp.stack([whole, swapped], 2), jnp.stack([swapped, whole], 2))
    weight = weight.reshape(width, kv)

    gain = norm_gain.astype(jnp.float32)[None, :]
    own = layer_input.astype(jnp.float32)
    own_rms = lax.rsqrt(jnp.mean(own * own, axis=-1, keepdims=True) + norm_eps)
    normed = (own * own_rms * gain).astype(jnp.bfloat16)
    scale = 1.0 / math.sqrt(tok_rows * loaders * columns)
    term = (
        lax.dot_general(normed, key_loader, (((0,), (0,)), ((), ())), preferred_element_type=jnp.float32)
        * scale
    ).astype(jnp.bfloat16)
    rows = width // (loaders * columns)
    term = term.reshape(8, 2, 8 * rows, kv)
    got = along_core(pick(term, 1 - core, 1))
    part = (pick(term, core, 1).astype(jnp.float32) + got.astype(jnp.float32)).astype(jnp.bfloat16)

    def reduce(part, axis, me, send):
        total = pick(part, me, axis).astype(jnp.float32)
        for n in (1, 3, 2):
            total = total + send(pick(part, (me + n) % 4, axis), n).astype(jnp.float32)
        return total

    part = reduce(part.reshape(8, 4, 2 * rows, kv), 1, yy, along_y).astype(jnp.bfloat16)
    part = part.reshape(2, 4, 2, rows, kv).transpose(0, 2, 1, 3, 4).reshape(4, 4, rows, kv)
    part = reduce(part, 0, zz, along_z).astype(jnp.bfloat16)
    weight_grad = reduce(part, 0, xx, along_x)

    packed = place_rows(to_loader, arrived)
    values = packed.astype(jnp.float32)
    inv_rms = lax.rsqrt(jnp.mean(values * values, axis=-1, keepdims=True) + norm_eps)
    input_delta = lax.dot_general(
        key_grad, weight, (((1,), (1,)), ((), ())), preferred_element_type=jnp.float32
    )
    scaled = input_delta * gain
    inner = jnp.mean(scaled * values, axis=-1, keepdims=True)
    input_grad = (inv_rms * (scaled - values * inv_rms * inv_rms * inner)).astype(jnp.bfloat16)
    return (input_grad, weight_grad)


def solution(mesh):
    return jax.shard_map(
        body,
        mesh=mesh,
        in_specs=(
            P(("dp", "fsdp"), None),
            P(("dp", "fsdp"), None),
            P(),
            P("fsdp", None),
            P("fsdp", None, None),
            P("fsdp", None, None),
            P("fsdp", None, None),
            P("fsdp", None, None),
            P("fsdp", None, None),
        ),
        out_specs=(P(("dp", "fsdp"), None), P(("dp", "fsdp"), None)),
        check_vma=False,
    )
```

time: 1120 us -> 420 us (0.38); the launches traced: 1100 us -> 418 us
  waiting for transfers between devices: 955 us -> 254 us
  matrix products: 21.6 us -> 57.9 us
  local copies, waits for them, and re-layouts: 57.9 us -> 27.3 us
  starting transfers between devices: 9.35 us -> 39.3 us
  between operations: 14.2 us -> 0.8 us
    reduce_scatter x1 -> x0, waiting for transfers between devices: 643 us -> none  [body(): lax.psum_scatter(lax.optimization_barrier((lax.dot_general(normed, key_gr...]
    all_to_all x1 -> x2, waiting for transfers between devices: 273 us -> 0.48 us  [exchange(): lax.all_to_all(blocks, 'dp', split_axis=0, concat_axis=0, tiled=True)]
    ppermute x0 -> x15, waiting for transfers between devices: none -> 253 us  [the longest x1 171 us: swap_zlo(): lax.ppermute(v, AXES, perm(lambda zh, x, c, y, zl: (zh, x, c, y, zl + 1)))]
    gather x2 -> x0, local copies, waits for them, and re-layouts: 56.1 us -> none  [the longest x1 32.4 us: body(): jnp.take(layer_input, send_rows.reshape(-1), axis=0)]
    all_gather x1 -> x0, waiting for transfers between devices: 38.8 us -> none  [body(): lax.all_gather(key_weight, 'fsdp', axis=0, tiled=True)]
    dot_general x2 -> x5, matrix products: 21.6 us -> 57.9 us  [the longest x1 22.1 us: place_rows(): lax.dot_general(matrix, rows, (((0,), (0,)), ((), ())), preferred_element...]
    ppermute x0 -> x15, starting transfers between devices: none -> 23.3 us  [the longest x6 11.1 us: along_y(): lax.ppermute(v, AXES, perm(lambda zh, x, c, y, zl: (zh, x, c, y + n, zl)))]
  transfers between devices with their start and end apart: 3 -> 17, of which waited for: 3 -> 8; matrix products, arithmetic and copies ran while one was open for 4% -> 18% of each run, Pallas kernels for 0% -> 0%
where the time goes in v1:
time: 420 us; the launch traced here: 418 us
  waiting for transfers between devices  254 us (60%)
  matrix products  57.9 us (14%)
  starting transfers between devices  39.3 us (9%)
  other arithmetic  38.9 us (9%)
  local copies, waits for them, and re-layouts  27.3 us (6%)
    ppermute x1, waiting for transfers between devices, swap_zlo(): lax.ppermute(v, AXES, perm(lambda zh, x, c, y, zl: (zh, x, c, y, zl + 1)))  171 us
    ppermute x6, waiting for transfers between devices, along_y(): lax.ppermute(v, AXES, perm(lambda zh, x, c, y, zl: (zh, x, c, y + n, zl)))  80.7 us
    dot_general x1, matrix products, place_rows(): lax.dot_general(matrix, rows, (((0,), (0,)), ((), ())), preferred_element...  22.1 us
    dot_general x2, matrix products, move(): jnp.dot(matrix, rows, preferred_element_type=jnp.float32)  16.9 us
    all_to_all x2, starting transfers between devices, exchange(): lax.all_to_all(blocks, 'dp', split_axis=0, concat_axis=0, tiled=True)  16 us
    convert_element_type x1, other arithmetic, body(): (inv_rms * (scaled - values * inv_rms * inv_rms * inner)).astype(jnp.bflo...  12.7 us
    ppermute x6, starting transfers between devices, along_y(): lax.ppermute(v, AXES, perm(lambda zh, x, c, y, zl: (zh, x, c, y + n, zl)))  11.1 us
    dot_general x1, matrix products, body(): lax.dot_general(normed, key_loader, (((0,), (0,)), ((), ())), preferred_e...  10.7 us
  transfers between devices with their start and end apart: 17, of which 8 were waited for; matrix products, arithmetic and copies ran while one was open for 18% of the time, Pallas kernels for 0%

profile of v1, /device:TPU:1, one launch (start us, length us, event | category | flops | bytes accessed | tf_op | source)
XLA Modules:
  0.0 417.8 jit_solution(3956212875708351816)
XLA Ops:
  3.7 2.7 fusion.37
  7.8 2.5 concatenate.24
  14.0 9.1 %all-to-all-start.1 = ((bf16[16,64,512]{2,1,0:T(8,128)(2,1)}), bf16[16,64,512]{2,1,0:T(8,128)(2,1)S(1)}, u32[]{:S(2)}, u32[]{:S(2)}) async-start(bf16[16,64,512]{2,1,0:T(8,128)(2,1)} %bitcast.87), calls=%async_computation.1 | async-start | bytes 2097152 | tf_op jit(solution)/shard_map/all_to_all | solution.py:135
  24.8 15.2 %convolution_convert_fusion = bf16[1024,8192]{1,0:T(8,128)(2,1)} fusion(bf16[512,8192]{1,0:T(8,128)(2,1)} %param.9, s32[1024]{0:T(1024)S(1)} %select_n.194), kind=kOutput, calls=%fused_computation.16 | convolution fusion | flops 8598847488 | bytes 25169920 | tf_op jit(solution)/shard_map/dot_general | solution.py:126
  40.5 6.9 %all-to-all-start = ((bf16[16,64,8192]{2,1,0:T(8,128)(2,1)}), bf16[16,64,8192]{2,1,0:T(8,128)(2,1)}, u32[]{:S(2)}, u32[]{:S(2)}) async-start(bf16[16,64,8192]{2,1,0:T(8,128)(2,1)} %bitcast.76), calls=%async_computation | async-start | bytes 33554432 | tf_op jit(solution)/shard_map/all_to_all | solution.py:135
  49.0 5.1 %fusion = f32[512]{0:T(512)S(1)} fusion(bf16[512,8192]{1,0:T(8,128)(2,1)} %param.9), kind=kLoop, calls=%fused_computation.5 | loop fusion | flops 12582400 | bytes 8390656 | tf_op jit(solution)/shard_map/reduce_sum | solution.py:156
  54.1 10.7 %multiply_convert_fusion = bf16[8192,512]{1,0:T(8,128)(2,1)} fusion(bf16[512,8192]{1,0:T(8,128)(2,1)} %param.9, f32[512]{0:T(512)S(1)} %add_rsqrt_fusion, f32[8192]{0:T(1024)S(1)} %convert_element_type.117, bf16[1024,512]{1,0:T(8,128)(2,1)S(1)} %bitcast.86, s32[1024]{0:T(1024)S(1)} %select_n.194), kind=kOutput, calls=%fused_computation.15 | convolution fusion | flops 4857790464 | bytes 17864704 | tf_op jit(solution)/shard_map/dot_general | solution.py:160
  64.9 4.5 %dynamic-slice_bitcast_fusion = bf16[8,512,512]{2,1,0:T(8,128)(2,1)} fusion(bf16[8,2,512,512]{3,2,1,0:T(8,128)(2,1)} %bitcast.79, s32[]{:T(128)S(6)} %select_n.213), kind=kLoop, calls=%fused_computation.23 | loop fusion | bytes 8388612 | tf_op jit(solution)/shard_map/jit(dynamic_index_in_dim)/squeeze | solution.py:56
  69.9 170.5 %collective-permute-done = bf16[512,512]{1,0:T(8,128)(2,1)S(1)} collective-permute-done((bf16[512,512]{1,0:T(8,128)(2,1)}, bf16[512,512]{1,0:T(8,128)(2,1)S(1)}, u32[]{:S(2)}, u32[]{:S(2)}) %collective-permute-start) | collective-permute-done | bytes 524320 | tf_op jit(solution)/shard_map/ppermute | solution.py:52
  245.1 2.3 broadcast_in_dim.18
  248.5 17.7 %collective-permute-done.1 = bf16[2,512,512]{2,1,0:T(8,128)(2,1)} collective-permute-done((bf16[2,512,512]{2,1,0:T(8,128)(2,1)S(1)}, bf16[2,512,512]{2,1,0:T(8,128)(2,1)}, u32[]{:S(2)}, u32[]{:S(2)}) %collective-permute-start.1) | collective-permute-done | bytes 1048608 | tf_op jit(solution)/shard_map/ppermute | solution.py:40
  268.5 2.3 bitcast_dynamic-update-slice_fusion.1
  270.8 19.0 %collective-permute-done.3 = bf16[2,512,512]{2,1,0:T(8,128)(2,1)} collective-permute-done((bf16[2,512,512]{2,1,0:T(8,128)(2,1)S(1)}, bf16[2,512,512]{2,1,0:T(8,128)(2,1)}, u32[]{:S(2)}, u32[]{:S(2)}) %collective-permute-start.3) | collective-permute-done | bytes 1048608 | tf_op jit(solution)/shard_map/ppermute | solution.py:40
  289.8 2.3 bitcast_dynamic-update-slice_fusion
  294.0 4.7 %fusion.11 = bf16[8,512,512]{2,1,0:T(8,128)(2,1)S(1)} fusion(bf16[8,512,512]{2,1,0:T(8,128)(2,1)} %collective-permute-done.5, bf16[8,2,512,512]{3,2,1,0:T(8,128)(2,1)} %bitcast.80, s32[]{:T(128)S(6)} %select_n.199), kind=kLoop, calls=%fused_computation.20 | loop fusion | flops 8388608 | bytes 12582916 | tf_op jit(solution)/shard_map/convert_element_type | solution.py:166
  302.7 4.2 collective-permute-start.8
  308.9 20.5 %collective-permute-done.6 = bf16[8,128,512]{2,1,0:T(8,128)(2,1)S(1)} collective-permute-done((bf16[8,128,512]{2,1,0:T(8,128)(2,1)}, bf16[8,128,512]{2,1,0:T(8,128)(2,1)S(1)}, u32[]{:S(2)}, u32[]{:S(2)}) %collective-permute-start.6) | collective-permute-done | bytes 1048608 | tf_op jit(solution)/shard_map/ppermute | solution.py:40
  329.4 23.6 %collective-permute-done.8 = bf16[8,128,512]{2,1,0:T(8,128)(2,1)} collective-permute-done((bf16[8,128,512]{2,1,0:T(8,128)(2,1)}, bf16[8,128,512]{2,1,0:T(8,128)(2,1)}, u32[]{:S(2)}, u32[]{:S(2)}) %collective-permute-start.8) | collective-permute-done | bytes 1048608 | tf_op jit(solution)/shard_map/ppermute | solution.py:40
  353.0 2.4 fusion.16
  356.4 2.6 collective-permute-start.11
  360.9 7.4 %maximum_select_fusion = bf16[4,2,2,512,512]{4,3,2,1,0:T(8,128)(2,1)S(1)} fusion(bf16[4,2,1,512,512]{4,3,2,1,0:T(8,128)(2,1)} %bitcast.14, bf16[4,2,1,512,512]{4,3,2,1,0:T(8,128)(2,1)} %bitcast.13, pred[]{:T(512)S(6)} %eq.82), kind=kLoop, calls=%fused_computation.18 | loop fusion | flops 12582912 | bytes 16777216 | tf_op jit(solution)/shard_map/jit(_where)/select_n | solution.py:151
  374.2 8.0 %fusion.39 = f32[512,8192]{1,0:T(8,128)} fusion(bf16[512,512]{1,0:T(8,128)(2,1)S(1)} %add_convert_fusion, bf16[8192,512]{1,0:T(8,128)(2,1)S(1)} %bitcast.75), kind=kOutput, calls=%fused_computation.93 | convolution fusion | flops 4294967296 | bytes 25690112 | tf_op jit(solution)/shard_map/dot_general | solution.py:182
  383.0 22.1 %fusion.3 = (f32[512]{0:T(512)S(1)}, f32[512]{0:T(512)S(1)}, bf16[512,8192]{1,0:T(8,128)(2,1)}) fusion(f32[512,8192]{1,0:T(8,128)} %fusion.39, f32[8192]{0:T(1024)S(1)} %convert_element_type.117, bf16[1024,8192]{1,0:T(8,128)(2,1)} %bitcast.4, s32[1024]{0:T(1024)S(1)} %select_n.191), kind=kOutput, calls=%fused_computation.8 | convolution fusion | flops 8619819008 | bytes 41984000 | tf_op jit(solution)/shard_map/dot_general | solution.py:129
  405.1 12.7 %fusion.8 = bf16[512,8192]{1,0:T(8,128)(2,1)} fusion(bf16[512,8192]{1,0:T(8,128)(2,1)} %get-tuple-element.31, f32[512,8192]{1,0:T(8,128)} %fusion.39, f32[512]{0:T(512)S(1)} %broadcast_multiply_fusion, f32[8192]{0:T(1024)S(1)} %convert_element_type.117, f32[512]{0:T(512)S(1)} %add_rsqrt_fusion.1), kind=kLoop, calls=%fused_computation.13 | loop fusion | flops 33554432 | bytes 33591296 | tf_op jit(solution)/shard_map/convert_element_type | solution.py:187
  (68 shorter events, 37.8 us)
Async XLA Ops:
  0.6 46.8 %copy-start = (bf16[1024,512]{1,0:T(8,128)(2,1)S(1)}, bf16[1024,512]{1,0:T(8,128)(2,1)}, u32[]{:S(2)}) copy-start(bf16[1024,512]{1,0:T(8,128)(2,1)} %param.12) | copy-start | bytes 3145732
  0.6 9.7 %copy-start.3 = (bf16[512,512]{1,0:T(8,128)(2,1)S(1)}, bf16[512,512]{1,0:T(8,128)(2,1)}, u32[]{:S(2)}) copy-start(bf16[512,512]{1,0:T(8,128)(2,1)} %param.10) | copy-start | bytes 1572868
  14.0 26.5 %all-to-all-start.1 = ((bf16[16,64,512]{2,1,0:T(8,128)(2,1)}), bf16[16,64,512]{2,1,0:T(8,128)(2,1)S(1)}, u32[]{:S(2)}, u32[]{:S(2)}) async-start(bf16[16,64,512]{2,1,0:T(8,128)(2,1)} %bitcast.87), calls=%async_computation.1 | async-start | bytes 2097152 | tf_op jit(solution)/shard_map/all_to_all | solution.py:135
  40.5 8.5 %copy-start.4 = (bf16[8192]{0:T(1024)(128)(2,1)S(1)}, bf16[8192]{0:T(1024)(128)(2,1)}, u32[]{:S(2)}) copy-start(bf16[8192]{0:T(1024)(128)(2,1)} %param.11) | copy-start | bytes 49156
  40.5 342.4 %all-to-all-start = ((bf16[16,64,8192]{2,1,0:T(8,128)(2,1)}), bf16[16,64,8192]{2,1,0:T(8,128)(2,1)}, u32[]{:S(2)}, u32[]{:S(2)}) async-start(bf16[16,64,8192]{2,1,0:T(8,128)(2,1)} %bitcast.76), calls=%async_computation | async-start | bytes 33554432 | tf_op jit(solution)/shard_map/all_to_all | solution.py:135
  48.3 192.1 %collective-permute-start = (bf16[512,512]{1,0:T(8,128)(2,1)}, bf16[512,512]{1,0:T(8,128)(2,1)S(1)}, u32[]{:S(2)}, u32[]{:S(2)}) collective-permute-start(bf16[512,512]{1,0:T(8,128)(2,1)} %fusion.47), channel_id=1, source_target_pairs={{0,1},{1,0},{2,3},{3,2},{4,5},{5,4},{6,7},{7,6},{8,9},{9,8},{10,11... | collective-permute-start | bytes 1572872 | tf_op jit(solution)/shard_map/ppermute | solution.py:52
  69.4 224.6 %collective-permute-start.5 = (bf16[8,512,512]{2,1,0:T(8,128)(2,1)}, bf16[8,512,512]{2,1,0:T(8,128)(2,1)}, u32[]{:S(2)}, u32[]{:S(2)}) collective-permute-start(bf16[8,512,512]{2,1,0:T(8,128)(2,1)} %dynamic-slice_bitcast_fusion), channel_id=1, source_target_pairs={{0,8},{1,9},{2,10},{3,11},{4,12},{5,13},{6,14},{7,15},{8,0},{9,1},... | collective-permute-start | bytes 12582920 | tf_op jit(solution)/shard_map/ppermute | solution.py:32
  240.6 25.6 %collective-permute-start.1 = (bf16[2,512,512]{2,1,0:T(8,128)(2,1)S(1)}, bf16[2,512,512]{2,1,0:T(8,128)(2,1)}, u32[]{:S(2)}, u32[]{:S(2)}) collective-permute-start(bf16[2,512,512]{2,1,0:T(8,128)(2,1)S(1)} %maximum_select_fusion.2), channel_id=1, source_target_pairs={{0,2},{1,3},{2,4},{3,5},{4,6},{5,7},{6,0},{7,1},{8,10},{9,11},{10,... | collective-permute-start | bytes 3145736 | tf_op jit(solution)/shard_map/ppermute | solution.py:40
  241.9 26.6 %collective-permute-start.2 = (bf16[2,512,512]{2,1,0:T(8,128)(2,1)S(1)}, bf16[2,512,512]{2,1,0:T(8,128)(2,1)}, u32[]{:S(2)}, u32[]{:S(2)}) collective-permute-start(bf16[2,512,512]{2,1,0:T(8,128)(2,1)S(1)} %maximum_select_fusion.2), channel_id=1, source_target_pairs={{0,6},{1,7},{2,0},{3,1},{4,2},{5,3},{6,4},{7,5},{8,14},{9,15},{10,... | collective-permute-start | bytes 3145736 | tf_op jit(solution)/shard_map/ppermute | solution.py:40
  243.5 46.3 %collective-permute-start.3 = (bf16[2,512,512]{2,1,0:T(8,128)(2,1)S(1)}, bf16[2,512,512]{2,1,0:T(8,128)(2,1)}, u32[]{:S(2)}, u32[]{:S(2)}) collective-permute-start(bf16[2,512,512]{2,1,0:T(8,128)(2,1)S(1)} %maximum_select_fusion.2), channel_id=1, source_target_pairs={{0,4},{1,5},{2,6},{3,7},{4,0},{5,1},{6,2},{7,3},{8,12},{9,13},{10,... | collective-permute-start | bytes 3145736 | tf_op jit(solution)/shard_map/ppermute | solution.py:40
  292.1 68.8 %collective-permute-start.4 = (bf16[4,2,512,512]{3,2,1,0:T(8,128)(2,1)}, bf16[4,2,512,512]{3,2,1,0:T(8,128)(2,1)}, u32[]{:S(2)}, u32[]{:S(2)}) collective-permute-start(bf16[4,2,512,512]{3,2,1,0:T(8,128)(2,1)} %bitcast_dynamic-update-slice_fusion), channel_id=1, source_target_pairs={{0,8},{1,9},{2,10},{3,11},{4,12},{5,13},{6,14},{7,15},{8,0},{9,1},... | collective-permute-start | bytes 12582920 | tf_op jit(solution)/shard_map/ppermute | solution.py:32
  298.7 2.0 copy-start.2
  302.2 27.2 %collective-permute-start.6 = (bf16[8,128,512]{2,1,0:T(8,128)(2,1)}, bf16[8,128,512]{2,1,0:T(8,128)(2,1)S(1)}, u32[]{:S(2)}, u32[]{:S(2)}) collective-permute-start(bf16[8,128,512]{2,1,0:T(8,128)(2,1)} %get-tuple-element.9), channel_id=1, source_target_pairs={{0,2},{1,3},{2,4},{3,5},{4,6},{5,7},{6,0},{7,1},{8,10},{9,11},{10,... | collective-permute-start | bytes 3145736 | tf_op jit(solution)/shard_map/ppermute | solution.py:40
  302.7 50.3 %collective-permute-start.8 = (bf16[8,128,512]{2,1,0:T(8,128)(2,1)}, bf16[8,128,512]{2,1,0:T(8,128)(2,1)}, u32[]{:S(2)}, u32[]{:S(2)}) collective-permute-start(bf16[8,128,512]{2,1,0:T(8,128)(2,1)} %get-tuple-element.10), channel_id=1, source_target_pairs={{0,4},{1,5},{2,6},{3,7},{4,0},{5,1},{6,2},{7,3},{8,12},{9,13},{10,... | collective-permute-start | bytes 3145736 | tf_op jit(solution)/shard_map/ppermute | solution.py:40
  306.8 46.1 %collective-permute-start.7 = (bf16[8,128,512]{2,1,0:T(8,128)(2,1)S(1)}, bf16[8,128,512]{2,1,0:T(8,128)(2,1)}, u32[]{:S(2)}, u32[]{:S(2)}) collective-permute-start(bf16[8,128,512]{2,1,0:T(8,128)(2,1)S(1)} %get-tuple-element.11), channel_id=1, source_target_pairs={{0,6},{1,7},{2,0},{3,1},{4,2},{5,3},{6,4},{7,5},{8,14},{9,15},{10,... | collective-permute-start | bytes 3145736 | tf_op jit(solution)/shard_map/ppermute | solution.py:40
  355.6 12.8 %collective-permute-start.9 = (bf16[4,64,512]{2,1,0:T(8,128)(2,1)S(1)}, bf16[4,64,512]{2,1,0:T(8,128)(2,1)S(1)}, u32[]{:S(2)}, u32[]{:S(2)}) collective-permute-start(bf16[4,64,512]{2,1,0:T(8,128)(2,1)S(1)} %get-tuple-element.12), channel_id=1, source_target_pairs={{0,1},{1,64},{2,3},{3,66},{4,5},{5,68},{6,7},{7,70},{8,9},{9,72},{... | collective-permute-start | bytes 786440 | tf_op jit(solution)/shard_map/ppermute | solution.py:48
  356.4 13.8 %collective-permute-start.11 = (bf16[4,64,512]{2,1,0:T(8,128)(2,1)S(1)}, bf16[4,64,512]{2,1,0:T(8,128)(2,1)S(1)}, u32[]{:S(2)}, u32[]{:S(2)}) collective-permute-start(bf16[4,64,512]{2,1,0:T(8,128)(2,1)S(1)} %get-tuple-element.13), channel_id=1, source_target_pairs={{0,64},{1,65},{2,66},{3,67},{4,68},{5,69},{6,70},{7,71},{8,72},{9,... | collective-permute-start | bytes 786440 | tf_op jit(solution)/shard_map/ppermute | solution.py:48
  359.0 11.3 %collective-permute-start.10 = (bf16[4,64,512]{2,1,0:T(8,128)(2,1)S(1)}, bf16[4,64,512]{2,1,0:T(8,128)(2,1)S(1)}, u32[]{:S(2)}, u32[]{:S(2)}) collective-permute-start(bf16[4,64,512]{2,1,0:T(8,128)(2,1)S(1)} %get-tuple-element.14), channel_id=1, source_target_pairs={{0,65},{1,0},{2,67},{3,2},{4,69},{5,4},{6,71},{7,6},{8,73},{9,8},{... | collective-permute-start | bytes 786440 | tf_op jit(solution)/shard_map/ppermute | solution.py:48
  370.4 11.8 %collective-permute-start.12 = (bf16[64,512]{1,0:T(8,128)(2,1)S(1)}, bf16[64,512]{1,0:T(8,128)(2,1)S(1)}, u32[]{:S(2)}, u32[]{:S(2)}) collective-permute-start(bf16[64,512]{1,0:T(8,128)(2,1)S(1)} %get-tuple-element.23), channel_id=1, source_target_pairs={{0,16},{1,17},{2,18},{3,19},{4,20},{5,21},{6,22},{7,23},{8,24},{9,... | collective-permute-start | bytes 196616 | tf_op jit(solution)/shard_map/ppermute | solution.py:36
  371.7 10.5 %collective-permute-start.14 = (bf16[64,512]{1,0:T(8,128)(2,1)S(1)}, bf16[64,512]{1,0:T(8,128)(2,1)S(1)}, u32[]{:S(2)}, u32[]{:S(2)}) collective-permute-start(bf16[64,512]{1,0:T(8,128)(2,1)S(1)} %get-tuple-element.24), channel_id=1, source_target_pairs={{0,32},{1,33},{2,34},{3,35},{4,36},{5,37},{6,38},{7,39},{8,40},{9,... | collective-permute-start | bytes 196616 | tf_op jit(solution)/shard_map/ppermute | solution.py:36
  374.0 8.3 %collective-permute-start.13 = (bf16[64,512]{1,0:T(8,128)(2,1)S(1)}, bf16[64,512]{1,0:T(8,128)(2,1)S(1)}, u32[]{:S(2)}, u32[]{:S(2)}) collective-permute-start(bf16[64,512]{1,0:T(8,128)(2,1)S(1)} %get-tuple-element.25), channel_id=1, source_target_pairs={{0,48},{1,49},{2,50},{3,51},{4,52},{5,53},{6,54},{7,55},{8,56},{9,... | collective-permute-start | bytes 196616 | tf_op jit(solution)/shard_map/ppermute | solution.py:36
  405.1 12.7 %copy-start.1 = (bf16[1024,512]{1,0:T(8,128)(2,1)S(1)}, bf16[1024,512]{1,0:T(8,128)(2,1)}, u32[]{:S(2)}) copy-start(bf16[1024,512]{1,0:T(8,128)(2,1)} %param.12) | copy-start | bytes 3145732

commit v2 on v1

--- a/solution.py
+++ b/solution.py
@@ -1,8 +1,11 @@
+import functools
 import math
 
 import jax
 import jax.numpy as jnp
 from jax import lax
+from jax.experimental import pallas as pl
+from jax.experimental.pallas import tpu as pltpu
 from jax.sharding import PartitionSpec as P
 
 HEAD = 128
@@ -56,19 +59,224 @@
     return lax.dynamic_index_in_dim(v, i, axis, keepdims=False)
 
 
-def rope_back(rotated, position):
+def rope_tables(position):
     half_head = HEAD // 2
     exponent = jnp.arange(half_head, dtype=jnp.float32) * (2.0 / HEAD)
     inverse = jnp.power(jnp.float32(rope_base), -exponent)
-    angle = position.astype(jnp.float32)[:, None] * inverse[None, :]
-    cosine = jnp.cos(angle)
-    sine = jnp.sin(angle)
-    cos_full = jnp.concatenate([cosine, cosine] * KV_HEADS, axis=1)
-    sin_full = jnp.concatenate([sine, -sine] * KV_HEADS, axis=1)
-    grads = rotated.astype(jnp.float32)
-    halves = [grads[:, i * half_head : (i + 1) * half_head] for i in range(2 * KV_HEADS)]
-    swapped = jnp.concatenate([halves[i ^ 1] for i in range(2 * KV_HEADS)], axis=1)
-    return (grads * cos_full + swapped * sin_full).astype(jnp.bfloat16)
+    angle = position.astype(jnp.float32)[:, None] * jnp.concatenate([inverse, inverse])[None, :]
+    sign = jnp.where(jnp.arange(HEAD) < half_head, 1.0, -1.0).astype(jnp.float32)
+    return jnp.cos(angle), jnp.sin(angle) * sign[None, :]
+
+
+def one_hot(select, count):
+    lanes = lax.broadcasted_iota(jnp.int32, (select.shape[0], count), 1)
+    return (select == lanes).astype(jnp.float32).astype(jnp.bfloat16)
+
+
+def rope_kernel(select_ref, cos_ref, sin_ref, rotated_ref, key_ref, out_ref):
+    cosine, sine = cos_ref[...], sin_ref[...]
+    for head in range(KV_HEADS):
+        cols = slice(head * HEAD, (head + 1) * HEAD)
+        grads = rotated_ref[:, cols].astype(jnp.float32)
+        turned = pltpu.roll(grads, HEAD // 2, 1)
+        key_ref[:, cols] = (grads * cosine + turned * sine).astype(jnp.bfloat16)
+    spread = one_hot(select_ref[...], key_ref.shape[0])
+    out_ref[...] = jnp.dot(spread, key_ref[...], preferred_element_type=jnp.float32).astype(jnp.bfloat16)
+
+
+def rope_and_spread(select, cosine, sine, rotated, beside):
+    rows, kv = rotated.shape
+    slots = select.shape[0]
+    whole = lambda j: (0, 0)
+    return pl.pallas_call(
+        rope_kernel,
+        grid=(1,),
+        in_specs=[pl.BlockSpec(v.shape, whole) for v in (select, cosine, sine, rotated)],
+        out_specs=[pl.BlockSpec((rows, kv), whole), pl.BlockSpec((slots, kv), lambda j: (0, beside // kv))],
+        out_shape=(
+            jax.ShapeDtypeStruct((rows, kv), jnp.bfloat16),
+            jax.ShapeDtypeStruct((slots, beside + kv), jnp.bfloat16),
+        ),
+        cost_estimate=pl.CostEstimate(flops=2 * slots * rows * kv, bytes_accessed=4 << 20, transcendentals=0),
+        compiler_params=pltpu.CompilerParams(vmem_limit_bytes=58 << 20),
+        name="rope_and_spread",
+    )(select, cosine, sine, rotated)
+
+
+BLOCK = 1024
+
+
+def spread_kernel(select_ref, rows_ref, *rest):
+    out_ref, spread = rest[-2:]
+
+    @pl.when(pl.program_id(0) == 0)
+    def _():
+        spread[...] = one_hot(select_ref[...], spread.shape[1])
+
+    out_ref[...] = jnp.dot(spread[...], rows_ref[...], preferred_element_type=jnp.float32).astype(jnp.bfloat16)
+
+
+def spread_rows(select, rows, first, width, beside=None):
+    slots, count = select.shape[0], rows.shape[0]
+    given = [] if beside is None else [beside]
+    total = width if beside is None else beside.shape[1]
+    return pl.pallas_call(
+        spread_kernel,
+        grid=(width // BLOCK,),
+        in_specs=[
+            pl.BlockSpec((slots, 1), lambda j: (0, 0)),
+            pl.BlockSpec((count, BLOCK), lambda j: (0, first // BLOCK + j)),
+        ]
+        + [pl.BlockSpec(memory_space=pl.ANY)] * len(given),
+        out_specs=pl.BlockSpec((slots, BLOCK), lambda j: (0, j)),
+        out_shape=jax.ShapeDtypeStruct((slots, total), jnp.bfloat16),
+        input_output_aliases={2: 0} if given else {},
+        scratch_shapes=[pltpu.VMEM((slots, count), jnp.bfloat16)],
+        cost_estimate=pl.CostEstimate(
+            flops=2 * slots * count * width, bytes_accessed=2 * (slots + count) * width, transcendentals=0
+        ),
+        compiler_params=pltpu.CompilerParams(vmem_limit_bytes=58 << 20),
+        name="spread_rows",
+    )(select, rows, *given)
+
+
+def lane_sums(values):
+    total = values[:, :128]
+    for k in range(1, values.shape[1] // 128):
+        total = total + values[:, k * 128 : (k + 1) * 128]
+    return total
+
+
+def delta_times_gain(key, weight, gain):
+    return lax.dot_general(key, weight, (((1,), (1,)), ((), ())), preferred_element_type=jnp.float32) * gain
+
+
+def first_pass_kernel(
+    core_ref, select_ref, arrived_ref, key_ref, mine_ref, other_ref, gain_ref, square_in, inner_in, *rest
+):
+    packed_ref, square_ref, inner_ref, gather = rest[-4:]
+
+    @pl.when(pl.program_id(0) == 0)
+    def _():
+        gather[...] = one_hot(select_ref[...], gather.shape[1])
+        square_ref[...] = square_in[...]
+        inner_ref[...] = inner_in[...]
+
+    values = jnp.dot(gather[...], arrived_ref[...], preferred_element_type=jnp.float32)
+    packed_ref[...] = values.astype(jnp.bfloat16)
+    square_ref[...] += lane_sums(values * values)
+    depth = mine_ref.shape[1]
+    core = core_ref[0]
+    for half, weight_ref in ((core, mine_ref), (1 - core, other_ref)):
+        cols = pl.ds(pl.multiple_of(half * depth, depth), depth)
+        scaled = delta_times_gain(key_ref[...], weight_ref[0], gain_ref[:, cols])
+        inner_ref[...] += lane_sums(scaled * packed_ref[:, cols].astype(jnp.float32))
+
+
+def first_pass(core, select, arrived, key_grad, mine, other, gain, square, inner, packed, first, part, width):
+    rows, kv = key_grad.shape
+    slots = arrived.shape[0]
+    depth = mine.shape[1]
+    base = first // BLOCK
+    whole = lambda j, core: (0, 0)
+    column = lambda j, core: (0, base + j)
+    deep = lambda j, core: (base + j, 0, 0)
+    sums = jax.ShapeDtypeStruct((rows, 128), jnp.float32)
+    operands = [core, select, arrived, key_grad, mine, other, gain, square, inner]
+    in_specs = [
+        pl.BlockSpec((rows, 1), whole),
+        pl.BlockSpec((slots, BLOCK), lambda j, core: (0, j)),
+        pl.BlockSpec((rows, kv), whole),
+        pl.BlockSpec((1, depth, kv), deep),
+        pl.BlockSpec((1, depth, kv), deep),
+        pl.BlockSpec((1, BLOCK), column),
+        pl.BlockSpec((rows, 128), whole),
+        pl.BlockSpec((rows, 128), whole),
+    ]
+    aliases = {}
+    if packed is not None:
+        operands.append(packed)
+        in_specs.append(pl.BlockSpec(memory_space=pl.ANY))
+        aliases = {9: 0}
+    return pl.pallas_call(
+        first_pass_kernel,
+        grid_spec=pltpu.PrefetchScalarGridSpec(
+            num_scalar_prefetch=1,
+            grid=(part // BLOCK,),
+            in_specs=in_specs,
+            out_specs=[
+                pl.BlockSpec((rows, BLOCK), column),
+                pl.BlockSpec((rows, 128), whole),
+                pl.BlockSpec((rows, 128), whole),
+            ],
+            scratch_shapes=[pltpu.VMEM((rows, slots), jnp.bfloat16)],
+        ),
+        out_shape=(jax.ShapeDtypeStruct((rows, width), jnp.bfloat16), sums, sums),
+        input_output_aliases=aliases,
+        cost_estimate=pl.CostEstimate(
+            flops=2 * rows * (slots + kv) * part,
+            bytes_accessed=2 * (slots + rows + kv) * part,
+            transcendentals=0,
+        ),
+        compiler_params=pltpu.CompilerParams(vmem_limit_bytes=58 << 20),
+        name="first_pass",
+    )(*operands)
+
+
+def second_pass_kernel(
+    core_ref, packed_ref, key_ref, mine_ref, other_ref, gain_ref, square_ref, inner_ref, out_ref, inv, coef, *, width
+):
+    @pl.when(pl.program_id(0) == 0)
+    def _():
+        square = jnp.sum(square_ref[...], axis=1, keepdims=True) * (1.0 / width)
+        inner = jnp.sum(inner_ref[...], axis=1, keepdims=True) * (1.0 / width)
+        inverse = lax.rsqrt(square + norm_eps)
+        inv[...] = inverse
+        coef[...] = inverse * inverse * inner
+
+    depth = mine_ref.shape[1]
+    core = core_ref[0]
+    for half, weight_ref in ((core, mine_ref), (1 - core, other_ref)):
+        cols = pl.ds(pl.multiple_of(half * depth, depth), depth)
+        scaled = delta_times_gain(key_ref[...], weight_ref[0], gain_ref[:, cols])
+        values = packed_ref[:, cols].astype(jnp.float32)
+        out_ref[:, cols] = (inv[...] * (scaled - values * coef[...])).astype(jnp.bfloat16)
+
+
+def second_pass(core, packed, key_grad, mine, other, gain, square, inner):
+    rows, kv = key_grad.shape
+    width = packed.shape[1]
+    depth = mine.shape[1]
+    whole = lambda j, core: (0, 0)
+    column = lambda j, core: (0, j)
+    deep = lambda j, core: (j, 0, 0)
+    return pl.pallas_call(
+        functools.partial(second_pass_kernel, width=width),
+        grid_spec=pltpu.PrefetchScalarGridSpec(
+            num_scalar_prefetch=1,
+            grid=(width // BLOCK,),
+            in_specs=[
+                pl.BlockSpec((rows, BLOCK), column),
+                pl.BlockSpec((rows, kv), whole),
+                pl.BlockSpec((1, depth, kv), deep),
+                pl.BlockSpec((1, depth, kv), deep),
+                pl.BlockSpec((1, BLOCK), column),
+                pl.BlockSpec((rows, 128), whole),
+                pl.BlockSpec((rows, 128), whole),
+            ],
+            out_specs=pl.BlockSpec((rows, BLOCK), column),
+            scratch_shapes=[pltpu.VMEM((rows, 1), jnp.float32), pltpu.VMEM((rows, 1), jnp.float32)],
+        ),
+        out_shape=jax.ShapeDtypeStruct((rows, width), jnp.bfloat16),
+        cost_estimate=pl.CostEstimate(
+            flops=2 * rows * kv * width, bytes_accessed=2 * (2 * rows + kv) * width, transcendentals=0
+        ),
+        compiler_params=pltpu.CompilerParams(vmem_limit_bytes=58 << 20),
+        name="second_pass",
+    )(core, packed, key_grad, mine, other, gain, square, inner)
+
+
+CHUNKS = (3072, 5120)
 
 
 def body(
@@ -110,6 +318,7 @@
         & (row_ids[:, None] < (arrive_start + arrive_length)[None, :])
     ).astype(jnp.int32)
     position = row_ids + jnp.sum(inside * (arrive_position - arrive_start)[None, :], axis=1)
+    slot = row_ids + jnp.sum(inside * (shard_ids * capacity - arrive_start)[None, :], axis=1)
 
     chosen = (pick(owners, dp)[None, :] == shard_ids[:, None]).astype(jnp.int32)
     send_start = jnp.sum(chosen * pick(source_offsets, dp)[None, :], axis=1)
@@ -117,42 +326,48 @@
 
     def spread(start, length):
         row = jnp.where(slot_ids[None, :] < length[:, None], start[:, None] + slot_ids[None, :], -1)
-        return (row.reshape(-1)[:, None] == row_ids[None, :]).astype(jnp.bfloat16)
+        return row.reshape(-1)[:, None]
 
     to_owner = spread(send_start, send_length)
     to_loader = spread(arrive_start, arrive_length)
-
-    def move(matrix, rows):
-        return jnp.dot(matrix, rows, preferred_element_type=jnp.float32).astype(jnp.bfloat16)
-
-    def place_rows(matrix, rows):
-        return lax.dot_general(
-            matrix, rows, (((0,), (0,)), ((), ())), preferred_element_type=jnp.float32
-        ).astype(jnp.bfloat16)
 
     def exchange(rows):
         blocks = rows.reshape(loaders, capacity, rows.shape[1])
         return lax.all_to_all(blocks, "dp", split_axis=0, concat_axis=0, tiled=True).reshape(rows.shape)
 
-    key_grad = rope_back(rotated_grad, position)
-    key_back = exchange(move(to_loader, key_grad))
-    arrived = exchange(move(to_owner, layer_input))
-    key_loader = place_rows(to_owner, key_back)
-
     depth = key_weight.shape[0] // 2
     half = pick(key_weight.reshape(2, depth, kv), core)
-    other = swap_zlo(half)
-    pair = jnp.where(zl == 0, jnp.stack([half, other]), jnp.stack([other, half]))
-    whole = jnp.zeros((4, 2, depth, kv), jnp.bfloat16)
-    whole = lax.dynamic_update_index_in_dim(whole, pair, yy, 0)
+    other_z = swap_zlo(half)
+
+    cosine, sine = rope_tables(position)
+    key_grad, message = rope_and_spread(to_loader, cosine, sine, rotated_grad, CHUNKS[0])
+    message = spread_rows(to_owner, layer_input, 0, CHUNKS[0], message)
+    outgoing = spread_rows(to_owner, layer_input, CHUNKS[0], CHUNKS[1])
+    message, other_z = lax.optimization_barrier((message, other_z))
+    arrived = [exchange(message)]
+
+    pair = jnp.where(zl == 0, jnp.stack([half, other_z]), jnp.stack([other_z, half]))
+    mine = jnp.zeros((4, 2, depth, kv), jnp.bfloat16)
+    mine = lax.dynamic_update_index_in_dim(mine, pair, yy, 0)
     for n in (1, 3, 2):
-        whole = lax.dynamic_update_index_in_dim(whole, along_y(pair, n), (yy - n) % 4, 0)
-    swapped = along_core(whole)
-    weight = jnp.where(core == 0, jnp.stack([whole, swapped], 2), jnp.stack([swapped, whole], 2))
-    weight = weight.reshape(width, kv)
+        mine = lax.dynamic_update_index_in_dim(mine, along_y(pair, n), (yy - n) % 4, 0)
+    mine = mine.reshape(8, depth, kv)
+    other = along_core(mine)
+
+    arrived[0], outgoing, later_input, mine, other = lax.optimization_barrier(
+        (arrived[0], outgoing, layer_input, mine, other)
+    )
+    arrived.append(exchange(outgoing))
+    key_back = arrived[0][:, CHUNKS[0] :]
+    key_loader = lax.dot_general(
+        (to_owner == row_ids[None, :]).astype(jnp.bfloat16),
+        key_back,
+        (((0,), (0,)), ((), ())),
+        preferred_element_type=jnp.float32,
+    ).astype(jnp.bfloat16)
 
     gain = norm_gain.astype(jnp.float32)[None, :]
-    own = layer_input.astype(jnp.float32)
+    own = later_input.astype(jnp.float32)
     own_rms = lax.rsqrt(jnp.mean(own * own, axis=-1, keepdims=True) + norm_eps)
     normed = (own * own_rms * gain).astype(jnp.bfloat16)
     scale = 1.0 / math.sqrt(tok_rows * loaders * columns)
@@ -176,15 +391,17 @@
     part = reduce(part, 0, zz, along_z).astype(jnp.bfloat16)
     weight_grad = reduce(part, 0, xx, along_x)
 
-    packed = place_rows(to_loader, arrived)
-    values = packed.astype(jnp.float32)
-    inv_rms = lax.rsqrt(jnp.mean(values * values, axis=-1, keepdims=True) + norm_eps)
-    input_delta = lax.dot_general(
-        key_grad, weight, (((1,), (1,)), ((), ())), preferred_element_type=jnp.float32
-    )
-    scaled = input_delta * gain
-    inner = jnp.mean(scaled * values, axis=-1, keepdims=True)
-    input_grad = (inv_rms * (scaled - values * inv_rms * inv_rms * inner)).astype(jnp.bfloat16)
+    core_id = jnp.reshape(core, (1,)).astype(jnp.int32)
+    select = slot[:, None]
+    square = jnp.zeros((tok_rows, 128), jnp.float32)
+    inner = jnp.zeros((tok_rows, 128), jnp.float32)
+    packed, first = None, 0
+    for rows_in, part in zip(arrived, CHUNKS):
+        packed, square, inner = first_pass(
+            core_id, select, rows_in, key_grad, mine, other, gain, square, inner, packed, first, part, width
+        )
+        first += part
+    input_grad = second_pass(core_id, packed, key_grad, mine, other, gain, square, inner)
     return (input_grad, weight_grad)
 
 

time: 420 us -> 318 us (0.76)
  waiting for transfers between devices: 254 us -> 159 us
  Pallas kernels: 0 us -> 58.2 us
  matrix products: 57.9 us -> 11 us
  other arithmetic: 38.9 us -> 18.3 us
  starting transfers between devices: 39.3 us -> 47.1 us
    ppermute x1, waiting for transfers between devices: 171 us -> 0.01 us  [swap_zlo(): lax.ppermute(v, AXES, perm(lambda zh, x, c, y, zl: (zh, x, c, y, zl + 1)))]
    pallas_call x0 -> x6, Pallas kernels: none -> 58.2 us  [the longest x2 22.5 us: first_pass(): pl.pallas_call(first_pass_kernel, grid_spec=pltpu.PrefetchScalarGridSpec(...]
    dot_general x4 -> x0, matrix products: 47.1 us -> none  [the longest x1 22.1 us: place_rows(): lax.dot_general(matrix, rows, (((0,), (0,)), ((), ())), preferred_element...]
    all_to_all x2, waiting for transfers between devices: 0.48 us -> 33.8 us  [exchange(): lax.all_to_all(blocks, 'dp', split_axis=0, concat_axis=0, tiled=True)]
    ppermute x3, waiting for transfers between devices: 1.87 us -> 34.9 us  [along_z(): return lax.ppermute(v, AXES, perm(step))]
    convert_element_type x3 -> x1, other arithmetic: 14.7 us -> 0.01 us  [rope_tables(): position.astype(jnp.float32)[:, None]]
    ppermute x3, starting transfers between devices: 3.76 us -> 15.9 us  [along_x(): lax.ppermute(v, AXES, perm(lambda zh, x, c, y, zl: (zh, x + n, c, y, zl)))]
    select_n x2, other arithmetic: 7.62 us -> 0.25 us  [the longest x1 0.17 us: body(): jnp.where(zl == 0, jnp.stack([half, other_z]), jnp.stack([other_z, half]))]
  transfers between devices with their start and end apart: 17 -> 17, of which waited for: 8 -> 9; matrix products, arithmetic and copies ran while one was open for 18% -> 16% of each run, Pallas kernels for 0% -> 10%
where the time goes in v2:
time: 318 us; the launch traced here: 317 us
  waiting for transfers between devices  159 us (50%)
  Pallas kernels  58.2 us (18%)
  starting transfers between devices  47.1 us (15%)
  local copies, waits for them, and re-layouts  23.2 us (7%)
  other arithmetic  18.3 us (6%)
  matrix products  11 us (3%)
    ppermute x6, waiting for transfers between devices, along_y(): lax.ppermute(v, AXES, perm(lambda zh, x, c, y, zl: (zh, x, c, y + n, zl)))  82.6 us
    ppermute x3, waiting for transfers between devices, along_z(): return lax.ppermute(v, AXES, perm(step))  34.9 us
    all_to_all x2, waiting for transfers between devices, exchange(): lax.all_to_all(blocks, 'dp', split_axis=0, concat_axis=0, tiled=True)  33.8 us
    pallas_call x2, Pallas kernels, first_pass(): pl.pallas_call(first_pass_kernel, grid_spec=pltpu.PrefetchScalarGridSpec(...  22.5 us
    pallas_call x2, Pallas kernels, spread_rows(): pl.pallas_call(spread_kernel, grid=(width // BLOCK,), in_specs=[pl.BlockS...  18.3 us
    ppermute x3, starting transfers between devices, along_x(): lax.ppermute(v, AXES, perm(lambda zh, x, c, y, zl: (zh, x + n, c, y, zl)))  15.9 us
    all_to_all x2, starting transfers between devices, exchange(): lax.all_to_all(blocks, 'dp', split_axis=0, concat_axis=0, tiled=True)  14.8 us
    pallas_call x1, Pallas kernels, second_pass(): pl.pallas_call(functools.partial(second_pass_kernel, width=width), grid_s...  14.1 us
  transfers between devices with their start and end apart: 17, of which 9 were waited for; matrix products, arithmetic and copies ran while one was open for 16% of the time, Pallas kernels for 10%

profile of v2, /device:TPU:1, one launch (start us, length us, event | category | flops | bytes accessed | tf_op | source)
XLA Modules:
  0.0 317.4 jit_solution(661401413745488724)
XLA Ops:
  1.9 2.5 collective-permute-start
  11.6 3.3 %rope_and_spread.1 = (bf16[512,512]{1,0:T(8,128)(2,1)}, bf16[1024,3584]{1,0:T(8,128)(2,1)}) custom-call(s32[1024,1]{1,0:T(8,128)} %select_n.242.select_ref, f32[512,128]{1,0:T(8,128)} %get-tuple-element.49.cos_ref, f32[512,128]{1,0:T(8,128)} %get-tuple-element.48.sin_ref, bf16[512,512]{1,0:T(8,128)(2,1)} %rotated_ref.1), custom_call_target="tpu_custom_call" | custom-call | flops 536870912 | bytes 4194304 | tf_op jit(solution)/shard_map/rope_and_spread/pallas_call | solution.py:91
  14.9 7.4 %spread_rows.2 = bf16[1024,3584]{1,0:T(8,128)(2,1)} custom-call(s32[1024,1]{1,0:T(8,128)} %select_n.243.select_ref, bf16[512,8192]{1,0:T(8,128)(2,1)} %rows_ref.3, bf16[1024,3584]{1,0:T(8,128)(2,1)} %get-tuple-element.17.rest_0_), custom_call_target="tpu_custom_call", output_to_operand_aliasing={{}: (2, {})} | custom-call | flops 3221225472 | bytes 9437184 | tf_op jit(solution)/shard_map/spread_rows/pallas_call | solution.py:123
  22.3 8.3 %all-to-all-start = ((bf16[16,64,3584]{2,1,0:T(8,128)(2,1)}), bf16[16,64,3584]{2,1,0:T(8,128)(2,1)}, u32[]{:S(2)}, u32[]{:S(2)}) async-start(bf16[16,64,3584]{2,1,0:T(8,128)(2,1)} %bitcast.70), calls=%async_computation | async-start | bytes 14680064 | tf_op jit(solution)/shard_map/all_to_all | solution.py:336
  38.8 18.1 %collective-permute-done.1 = bf16[2,512,512]{2,1,0:T(8,128)(2,1)} collective-permute-done((bf16[2,512,512]{2,1,0:T(8,128)(2,1)S(1)}, bf16[2,512,512]{2,1,0:T(8,128)(2,1)}, u32[]{:S(2)}, u32[]{:S(2)}) %collective-permute-start.1) | collective-permute-done | bytes 1048608 | tf_op jit(solution)/shard_map/ppermute | solution.py:43
  61.4 19.0 %collective-permute-done.3 = bf16[2,512,512]{2,1,0:T(8,128)(2,1)} collective-permute-done((bf16[2,512,512]{2,1,0:T(8,128)(2,1)S(1)}, bf16[2,512,512]{2,1,0:T(8,128)(2,1)}, u32[]{:S(2)}, u32[]{:S(2)}) %collective-permute-start.3) | collective-permute-done | bytes 1048608 | tf_op jit(solution)/shard_map/ppermute | solution.py:43
  84.3 10.9 %spread_rows.3 = bf16[1024,5120]{1,0:T(8,128)(2,1)} custom-call(s32[1024,1]{1,0:T(8,128)} %select_n.243.select_ref, bf16[512,8192]{1,0:T(8,128)(2,1)} %rows_ref.3), custom_call_target="tpu_custom_call" | custom-call | flops 5368709120 | bytes 15728640 | tf_op jit(solution)/shard_map/spread_rows/pallas_call | solution.py:123
  95.2 33.8 %all-to-all-done = bf16[16,64,3584]{2,1,0:T(8,128)(2,1)} async-done(((bf16[16,64,3584]{2,1,0:T(8,128)(2,1)}), bf16[16,64,3584]{2,1,0:T(8,128)(2,1)}, u32[]{:S(2)}, u32[]{:S(2)}) %all-to-all-start) | async-done | bytes 7340064 | tf_op jit(solution)/shard_map/all_to_all | solution.py:336
  128.9 6.5 %all-to-all-start.1 = ((bf16[16,64,5120]{2,1,0:T(8,128)(2,1)}), bf16[16,64,5120]{2,1,0:T(8,128)(2,1)}, u32[]{:S(2)}, u32[]{:S(2)}) async-start(bf16[16,64,5120]{2,1,0:T(8,128)(2,1)} %bitcast.73), calls=%async_computation.1 | async-start | bytes 20971520 | tf_op jit(solution)/shard_map/all_to_all | solution.py:336
  135.4 5.1 %fusion = f32[512]{0:T(512)S(1)} fusion(bf16[512,8192]{1,0:T(8,128)(2,1)} %rows_ref.3), kind=kLoop, calls=%fused_computation.2 | loop fusion | flops 12582400 | bytes 8390656 | tf_op jit(solution)/shard_map/reduce_sum | solution.py:371
  140.5 11.0 %multiply_convert_fusion = bf16[8192,512]{1,0:T(8,128)(2,1)} fusion(bf16[512,8192]{1,0:T(8,128)(2,1)} %rows_ref.3, f32[8192]{0:T(1024)S(1)} %convert_element_type.90, f32[512]{0:T(512)S(1)} %add_rsqrt_fusion, bf16[1024,3584]{1,0:T(8,128)(2,1)} %bitcast.8.arrived_ref, s32[1024]{0:T(1024)S(1)} %select_n.217), kind=kOutput, calls=%fused_computation.5 | convolution fusion | flops 4857790464 | bytes 17864704 | tf_op jit(solution)/shard_map/dot_general | solution.py:375
  151.6 4.4 %dynamic-slice_bitcast_fusion = bf16[8,512,512]{2,1,0:T(8,128)(2,1)} fusion(bf16[8,2,512,512]{3,2,1,0:T(8,128)(2,1)} %bitcast.74, s32[]{:T(128)S(6)} %select_n.218), kind=kLoop, calls=%fused_computation.10 | loop fusion | bytes 8388612 | tf_op jit(solution)/shard_map/jit(dynamic_index_in_dim)/squeeze | solution.py:59
  156.2 7.3 %collective-permute-done.5 = bf16[8,512,512]{2,1,0:T(8,128)(2,1)} collective-permute-done((bf16[8,512,512]{2,1,0:T(8,128)(2,1)}, bf16[8,512,512]{2,1,0:T(8,128)(2,1)}, u32[]{:S(2)}, u32[]{:S(2)}) %collective-permute-start.5) | collective-permute-done | bytes 4194336 | tf_op jit(solution)/shard_map/ppermute | solution.py:35
  163.5 4.7 %fusion.4 = bf16[8,512,512]{2,1,0:T(8,128)(2,1)S(1)} fusion(bf16[8,512,512]{2,1,0:T(8,128)(2,1)} %collective-permute-done.5, bf16[8,2,512,512]{3,2,1,0:T(8,128)(2,1)} %bitcast.75, s32[]{:T(128)S(6)} %select_n.203), kind=kLoop, calls=%fused_computation.7 | loop fusion | flops 8388608 | bytes 12582916 | tf_op jit(solution)/shard_map/convert_element_type | solution.py:381
  175.8 21.9 %collective-permute-done.6 = bf16[8,128,512]{2,1,0:T(8,128)(2,1)S(1)} collective-permute-done((bf16[8,128,512]{2,1,0:T(8,128)(2,1)}, bf16[8,128,512]{2,1,0:T(8,128)(2,1)S(1)}, u32[]{:S(2)}, u32[]{:S(2)}) %collective-permute-start.6) | collective-permute-done | bytes 1048608 | tf_op jit(solution)/shard_map/ppermute | solution.py:43
  197.7 23.6 %collective-permute-done.8 = bf16[8,128,512]{2,1,0:T(8,128)(2,1)} collective-permute-done((bf16[8,128,512]{2,1,0:T(8,128)(2,1)S(1)}, bf16[8,128,512]{2,1,0:T(8,128)(2,1)}, u32[]{:S(2)}, u32[]{:S(2)}) %collective-permute-start.8) | collective-permute-done | bytes 1048608 | tf_op jit(solution)/shard_map/ppermute | solution.py:43
  221.2 2.4 fusion.9
  228.4 25.9 %collective-permute-done.10 = bf16[4,64,512]{2,1,0:T(8,128)(2,1)S(1)} collective-permute-done((bf16[4,64,512]{2,1,0:T(8,128)(2,1)S(1)}, bf16[4,64,512]{2,1,0:T(8,128)(2,1)S(1)}, u32[]{:S(2)}, u32[]{:S(2)}) %collective-permute-start.10) | collective-permute-done | bytes 262176 | tf_op jit(solution)/shard_map/ppermute | solution.py:51
  254.3 3.0 collective-permute-done.11
  257.3 6.0 %collective-permute-done.9 = bf16[4,64,512]{2,1,0:T(8,128)(2,1)S(1)} collective-permute-done((bf16[4,64,512]{2,1,0:T(8,128)(2,1)S(1)}, bf16[4,64,512]{2,1,0:T(8,128)(2,1)S(1)}, u32[]{:S(2)}, u32[]{:S(2)}) %collective-permute-start.9) | collective-permute-done | bytes 262176 | tf_op jit(solution)/shard_map/ppermute | solution.py:51
  266.4 12.9 %collective-permute-start.14 = (bf16[64,512]{1,0:T(8,128)(2,1)S(1)}, bf16[64,512]{1,0:T(8,128)(2,1)S(1)}, u32[]{:S(2)}, u32[]{:S(2)}) collective-permute-start(bf16[64,512]{1,0:T(8,128)(2,1)S(1)} %get-tuple-element.46), channel_id=1, source_target_pairs={{0,32},{1,33},{2,34},{3,35},{4,36},{5,37},{6,38},{7,39},{8,40},{9,... | collective-permute-start | bytes 196616 | tf_op jit(solution)/shard_map/ppermute | solution.py:39
  280.1 9.6 %first_pass.2 = (bf16[512,8192]{1,0:T(8,128)(2,1)}, f32[512,128]{1,0:T(8,128)}, f32[512,128]{1,0:T(8,128)}) custom-call(s32[1]{0:T(128)} %bitcast.core_ref, s32[512,1]{1,0:T(8,128)} %iota_add_fusion.select_ref, bf16[1024,3584]{1,0:T(8,128)(2,1)} %bitcast.8.arrived_ref, bf16[512,512]{1,0:T(8,128)(2,1)} %get-tuple-element.21.key_ref, ...), custom_call_target="tpu_custom_call" | custom-call | flops 4831838208 | bytes 12582912 | tf_op jit(solution)/shard_map/first_pass/pallas_call | solution.py:201
  290.4 12.9 %first_pass.3 = (bf16[512,8192]{1,0:T(8,128)(2,1)}, f32[512,128]{1,0:T(8,128)}, f32[512,128]{1,0:T(8,128)}) custom-call(s32[1]{0:T(128)} %bitcast.core_ref, s32[512,1]{1,0:T(8,128)} %iota_add_fusion.select_ref, bf16[1024,5120]{1,0:T(8,128)(2,1)} %bitcast.17.arrived_ref, bf16[512,512]{1,0:T(8,128)(2,1)} %get-tuple-element.21.key_ref, ...), custom_call_target="tpu_custom_call", output_to_operand_aliasing={{0}: (9, {})} | custom-call | flops 8053063680 | bytes 20971520 | tf_op jit(solution)/shard_map/first_pass/pallas_call | solution.py:201
  303.4 14.1 %second_pass.1 = bf16[512,8192]{1,0:T(8,128)(2,1)} custom-call(s32[1]{0:T(128)} %bitcast.core_ref, bf16[512,8192]{1,0:T(8,128)(2,1)} %get-tuple-element.28.packed_ref, bf16[512,512]{1,0:T(8,128)(2,1)} %get-tuple-element.21.key_ref, bf16[8,512,512]{2,1,0:T(8,128)(2,1)} %bitcast.15.mine_ref, bf16[8,512,512]{2,1,0:T(8,128)(2,1)} %collective-permute-done.4.other_ref, ...), custom_call_target="tpu_custom_call" | custom-call | flops 4294967296 | bytes 25165824 | tf_op jit(solution)/shard_map/second_pass/pallas_call | solution.py:253
  (66 shorter events, 41.8 us)
Async XLA Ops:
  0.6 1.2 copy-start
  1.9 20.4 %collective-permute-start = (bf16[512,512]{1,0:T(8,128)(2,1)S(1)}, bf16[512,512]{1,0:T(8,128)(2,1)S(1)}, u32[]{:S(2)}, u32[]{:S(2)}) collective-permute-start(bf16[512,512]{1,0:T(8,128)(2,1)S(1)} %fusion.28), channel_id=1, source_target_pairs={{0,1},{1,0},{2,3},{3,2},{4,5},{5,4},{6,7},{7,6},{8,9},{9,8},{10,11... | collective-permute-start | bytes 1572872 | tf_op jit(solution)/shard_map/ppermute | solution.py:55
  22.3 106.7 %all-to-all-start = ((bf16[16,64,3584]{2,1,0:T(8,128)(2,1)}), bf16[16,64,3584]{2,1,0:T(8,128)(2,1)}, u32[]{:S(2)}, u32[]{:S(2)}) async-start(bf16[16,64,3584]{2,1,0:T(8,128)(2,1)} %bitcast.70), calls=%async_computation | async-start | bytes 14680064 | tf_op jit(solution)/shard_map/all_to_all | solution.py:336
  30.8 26.1 %collective-permute-start.1 = (bf16[2,512,512]{2,1,0:T(8,128)(2,1)S(1)}, bf16[2,512,512]{2,1,0:T(8,128)(2,1)}, u32[]{:S(2)}, u32[]{:S(2)}) collective-permute-start(bf16[2,512,512]{2,1,0:T(8,128)(2,1)S(1)} %maximum_select_fusion.1), channel_id=1, source_target_pairs={{0,2},{1,3},{2,4},{3,5},{4,6},{5,7},{6,0},{7,1},{8,10},{9,11},{10,... | collective-permute-start | bytes 3145736 | tf_op jit(solution)/shard_map/ppermute | solution.py:43
  32.2 27.0 %collective-permute-start.2 = (bf16[2,512,512]{2,1,0:T(8,128)(2,1)S(1)}, bf16[2,512,512]{2,1,0:T(8,128)(2,1)}, u32[]{:S(2)}, u32[]{:S(2)}) collective-permute-start(bf16[2,512,512]{2,1,0:T(8,128)(2,1)S(1)} %maximum_select_fusion.1), channel_id=1, source_target_pairs={{0,6},{1,7},{2,0},{3,1},{4,2},{5,3},{6,4},{7,5},{8,14},{9,15},{10,... | collective-permute-start | bytes 3145736 | tf_op jit(solution)/shard_map/ppermute | solution.py:43
  33.7 46.8 %collective-permute-start.3 = (bf16[2,512,512]{2,1,0:T(8,128)(2,1)S(1)}, bf16[2,512,512]{2,1,0:T(8,128)(2,1)}, u32[]{:S(2)}, u32[]{:S(2)}) collective-permute-start(bf16[2,512,512]{2,1,0:T(8,128)(2,1)S(1)} %maximum_select_fusion.1), channel_id=1, source_target_pairs={{0,4},{1,5},{2,6},{3,7},{4,0},{5,1},{6,2},{7,3},{8,12},{9,13},{10,... | collective-permute-start | bytes 3145736 | tf_op jit(solution)/shard_map/ppermute | solution.py:43
  37.6 46.6 %copy-start.4 = (bf16[8192]{0:T(1024)(128)(2,1)S(1)}, bf16[8192]{0:T(1024)(128)(2,1)}, u32[]{:S(2)}) copy-start(bf16[8192]{0:T(1024)(128)(2,1)} %param.11) | copy-start | bytes 49156
  82.8 12.3 %collective-permute-start.4 = (bf16[8,512,512]{2,1,0:T(8,128)(2,1)}, bf16[8,512,512]{2,1,0:T(8,128)(2,1)}, u32[]{:S(2)}, u32[]{:S(2)}) collective-permute-start(bf16[8,512,512]{2,1,0:T(8,128)(2,1)} %bitcast.15.mine_ref), channel_id=1, source_target_pairs={{0,8},{1,9},{2,10},{3,11},{4,12},{5,13},{6,14},{7,15},{8,0},{9,1},... | collective-permute-start | bytes 12582920 | tf_op jit(solution)/shard_map/ppermute | solution.py:35
  84.3 56.3 %copy-start.3 = (f32[8192]{0:T(1024)}, f32[8192]{0:T(1024)S(1)}, u32[]{:S(2)}) copy-start(f32[8192]{0:T(1024)S(1)} %convert_element_type.90) | copy-start | bytes 98308
  128.9 161.5 %all-to-all-start.1 = ((bf16[16,64,5120]{2,1,0:T(8,128)(2,1)}), bf16[16,64,5120]{2,1,0:T(8,128)(2,1)}, u32[]{:S(2)}, u32[]{:S(2)}) async-start(bf16[16,64,5120]{2,1,0:T(8,128)(2,1)} %bitcast.73), calls=%async_computation.1 | async-start | bytes 20971520 | tf_op jit(solution)/shard_map/all_to_all | solution.py:336
  156.0 7.5 %collective-permute-start.5 = (bf16[8,512,512]{2,1,0:T(8,128)(2,1)}, bf16[8,512,512]{2,1,0:T(8,128)(2,1)}, u32[]{:S(2)}, u32[]{:S(2)}) collective-permute-start(bf16[8,512,512]{2,1,0:T(8,128)(2,1)} %dynamic-slice_bitcast_fusion), channel_id=1, source_target_pairs={{0,8},{1,9},{2,10},{3,11},{4,12},{5,13},{6,14},{7,15},{8,0},{9,1},... | collective-permute-start | bytes 12582920 | tf_op jit(solution)/shard_map/ppermute | solution.py:35
  168.2 2.0 copy-start.2
  171.4 26.3 %collective-permute-start.6 = (bf16[8,128,512]{2,1,0:T(8,128)(2,1)}, bf16[8,128,512]{2,1,0:T(8,128)(2,1)S(1)}, u32[]{:S(2)}, u32[]{:S(2)}) collective-permute-start(bf16[8,128,512]{2,1,0:T(8,128)(2,1)} %get-tuple-element.39), channel_id=1, source_target_pairs={{0,2},{1,3},{2,4},{3,5},{4,6},{5,7},{6,0},{7,1},{8,10},{9,11},{10,... | collective-permute-start | bytes 3145736 | tf_op jit(solution)/shard_map/ppermute | solution.py:43
  172.7 25.0 %collective-permute-start.7 = (bf16[8,128,512]{2,1,0:T(8,128)(2,1)S(1)}, bf16[8,128,512]{2,1,0:T(8,128)(2,1)}, u32[]{:S(2)}, u32[]{:S(2)}) collective-permute-start(bf16[8,128,512]{2,1,0:T(8,128)(2,1)S(1)} %get-tuple-element.41), channel_id=1, source_target_pairs={{0,6},{1,7},{2,0},{3,1},{4,2},{5,3},{6,4},{7,5},{8,14},{9,15},{10,... | collective-permute-start | bytes 3145736 | tf_op jit(solution)/shard_map/ppermute | solution.py:43
  174.1 47.1 %collective-permute-start.8 = (bf16[8,128,512]{2,1,0:T(8,128)(2,1)S(1)}, bf16[8,128,512]{2,1,0:T(8,128)(2,1)}, u32[]{:S(2)}, u32[]{:S(2)}) collective-permute-start(bf16[8,128,512]{2,1,0:T(8,128)(2,1)S(1)} %get-tuple-element.40), channel_id=1, source_target_pairs={{0,4},{1,5},{2,6},{3,7},{4,0},{5,1},{6,2},{7,3},{8,12},{9,13},{10,... | collective-permute-start | bytes 3145736 | tf_op jit(solution)/shard_map/ppermute | solution.py:43
  223.9 30.4 %collective-permute-start.10 = (bf16[4,64,512]{2,1,0:T(8,128)(2,1)S(1)}, bf16[4,64,512]{2,1,0:T(8,128)(2,1)S(1)}, u32[]{:S(2)}, u32[]{:S(2)}) collective-permute-start(bf16[4,64,512]{2,1,0:T(8,128)(2,1)S(1)} %get-tuple-element.44), channel_id=1, source_target_pairs={{0,65},{1,0},{2,67},{3,2},{4,69},{5,4},{6,71},{7,6},{8,73},{9,8},{... | collective-permute-start | bytes 786440 | tf_op jit(solution)/shard_map/ppermute | solution.py:51
  225.5 31.8 %collective-permute-start.11 = (bf16[4,64,512]{2,1,0:T(8,128)(2,1)S(1)}, bf16[4,64,512]{2,1,0:T(8,128)(2,1)S(1)}, u32[]{:S(2)}, u32[]{:S(2)}) collective-permute-start(bf16[4,64,512]{2,1,0:T(8,128)(2,1)S(1)} %get-tuple-element.43), channel_id=1, source_target_pairs={{0,64},{1,65},{2,66},{3,67},{4,68},{5,69},{6,70},{7,71},{8,72},{9,... | collective-permute-start | bytes 786440 | tf_op jit(solution)/shard_map/ppermute | solution.py:51
  226.7 36.6 %collective-permute-start.9 = (bf16[4,64,512]{2,1,0:T(8,128)(2,1)S(1)}, bf16[4,64,512]{2,1,0:T(8,128)(2,1)S(1)}, u32[]{:S(2)}, u32[]{:S(2)}) collective-permute-start(bf16[4,64,512]{2,1,0:T(8,128)(2,1)S(1)} %get-tuple-element.42), channel_id=1, source_target_pairs={{0,1},{1,64},{2,3},{3,66},{4,5},{5,68},{6,7},{7,70},{8,9},{9,72},{... | collective-permute-start | bytes 786440 | tf_op jit(solution)/shard_map/ppermute | solution.py:51
  263.4 26.3 %collective-permute-start.12 = (bf16[64,512]{1,0:T(8,128)(2,1)S(1)}, bf16[64,512]{1,0:T(8,128)(2,1)S(1)}, u32[]{:S(2)}, u32[]{:S(2)}) collective-permute-start(bf16[64,512]{1,0:T(8,128)(2,1)S(1)} %get-tuple-element.45), channel_id=1, source_target_pairs={{0,16},{1,17},{2,18},{3,19},{4,20},{5,21},{6,22},{7,23},{8,24},{9,... | collective-permute-start | bytes 196616 | tf_op jit(solution)/shard_map/ppermute | solution.py:39
  264.7 25.0 %collective-permute-start.13 = (bf16[64,512]{1,0:T(8,128)(2,1)S(1)}, bf16[64,512]{1,0:T(8,128)(2,1)S(1)}, u32[]{:S(2)}, u32[]{:S(2)}) collective-permute-start(bf16[64,512]{1,0:T(8,128)(2,1)S(1)} %get-tuple-element.47), channel_id=1, source_target_pairs={{0,48},{1,49},{2,50},{3,51},{4,52},{5,53},{6,54},{7,55},{8,56},{9,... | collective-permute-start | bytes 196616 | tf_op jit(solution)/shard_map/ppermute | solution.py:39
  266.4 23.3 %collective-permute-start.14 = (bf16[64,512]{1,0:T(8,128)(2,1)S(1)}, bf16[64,512]{1,0:T(8,128)(2,1)S(1)}, u32[]{:S(2)}, u32[]{:S(2)}) collective-permute-start(bf16[64,512]{1,0:T(8,128)(2,1)S(1)} %get-tuple-element.46), channel_id=1, source_target_pairs={{0,32},{1,33},{2,34},{3,35},{4,36},{5,37},{6,38},{7,39},{8,40},{9,... | collective-permute-start | bytes 196616 | tf_op jit(solution)/shard_map/ppermute | solution.py:39
  303.4 14.1 %copy-start.1 = (bf16[1024,512]{1,0:T(8,128)(2,1)S(1)}, bf16[1024,512]{1,0:T(8,128)(2,1)}, u32[]{:S(2)}) copy-start(bf16[1024,512]{1,0:T(8,128)(2,1)} %param.12) | copy-start | bytes 3145732

commit v3 on v2

--- a/solution.py
+++ b/solution.py
@@ -147,133 +147,172 @@
     return total
 
 
-def delta_times_gain(key, weight, gain):
-    return lax.dot_general(key, weight, (((1,), (1,)), ((), ())), preferred_element_type=jnp.float32) * gain
-
-
-def first_pass_kernel(
-    core_ref, select_ref, arrived_ref, key_ref, mine_ref, other_ref, gain_ref, square_in, inner_in, *rest
-):
-    packed_ref, square_ref, inner_ref, gather = rest[-4:]
-
-    @pl.when(pl.program_id(0) == 0)
-    def _():
-        gather[...] = one_hot(select_ref[...], gather.shape[1])
-        square_ref[...] = square_in[...]
-        inner_ref[...] = inner_in[...]
-
-    values = jnp.dot(gather[...], arrived_ref[...], preferred_element_type=jnp.float32)
-    packed_ref[...] = values.astype(jnp.bfloat16)
-    square_ref[...] += lane_sums(values * values)
+def delta_kernel(core_ref, key_ref, mine_ref, other_ref, gain_ref, out_ref):
     depth = mine_ref.shape[1]
     core = core_ref[0]
     for half, weight_ref in ((core, mine_ref), (1 - core, other_ref)):
         cols = pl.ds(pl.multiple_of(half * depth, depth), depth)
-        scaled = delta_times_gain(key_ref[...], weight_ref[0], gain_ref[:, cols])
-        inner_ref[...] += lane_sums(scaled * packed_ref[:, cols].astype(jnp.float32))
-
-
-def first_pass(core, select, arrived, key_grad, mine, other, gain, square, inner, packed, first, part, width):
+        delta = lax.dot_general(
+            key_ref[...], weight_ref[0], (((1,), (1,)), ((), ())), preferred_element_type=jnp.float32
+        )
+        out_ref[:, cols] = delta * gain_ref[:, cols]
+
+
+def scaled_delta(core, key_grad, mine, other, gain):
     rows, kv = key_grad.shape
-    slots = arrived.shape[0]
-    depth = mine.shape[1]
+    count, depth = mine.shape[0], mine.shape[1]
+    width = gain.shape[1]
+    return pl.pallas_call(
+        delta_kernel,
+        grid_spec=pltpu.PrefetchScalarGridSpec(
+            num_scalar_prefetch=1,
+            grid=(count,),
+            in_specs=[
+                pl.BlockSpec((rows, kv), lambda j, core: (0, 0)),
+                pl.BlockSpec((1, depth, kv), lambda j, core: (j, 0, 0)),
+                pl.BlockSpec((1, depth, kv), lambda j, core: (j, 0, 0)),
+                pl.BlockSpec((1, 2 * depth), lambda j, core: (0, j)),
+            ],
+            out_specs=pl.BlockSpec((rows, 2 * depth), lambda j, core: (0, j)),
+        ),
+        out_shape=jax.ShapeDtypeStruct((rows, width), jnp.float32),
+        cost_estimate=pl.CostEstimate(
+            flops=2 * rows * kv * width, bytes_accessed=(4 * rows + 2 * kv) * width, transcendentals=0
+        ),
+        compiler_params=pltpu.CompilerParams(vmem_limit_bytes=58 << 20),
+        name="scaled_delta",
+    )(core, key_grad, mine, other, gain)
+
+
+def place_and_sum(gather, arrived_ref, scaled_ref, square_ref, inner_ref):
+    values = jnp.dot(gather[...], arrived_ref[...], preferred_element_type=jnp.float32)
+    square_ref[...] += lane_sums(values * values)
+    inner_ref[...] += lane_sums(scaled_ref[...] * values)
+    return values.astype(jnp.bfloat16)
+
+
+def first_pass_kernel(select_ref, arrived_ref, scaled_ref, square_in, inner_in, *rest):
+    packed_ref, square_ref, inner_ref, gather = rest[-4:]
+
+    @pl.when(pl.program_id(0) == 0)
+    def _():
+        gather[...] = one_hot(select_ref[...], gather.shape[1])
+        square_ref[...] = square_in[...]
+        inner_ref[...] = inner_in[...]
+
+    packed_ref[...] = place_and_sum(gather, arrived_ref, scaled_ref, square_ref, inner_ref)
+
+
+def first_pass(select, arrived, scaled, square, inner, packed, first, part, total):
+    rows, slots = select.shape[0], arrived.shape[0]
     base = first // BLOCK
-    whole = lambda j, core: (0, 0)
-    column = lambda j, core: (0, base + j)
-    deep = lambda j, core: (base + j, 0, 0)
+    whole = lambda j: (0, 0)
+    column = lambda j: (0, base + j)
     sums = jax.ShapeDtypeStruct((rows, 128), jnp.float32)
-    operands = [core, select, arrived, key_grad, mine, other, gain, square, inner]
+    operands = [select, arrived, scaled, square, inner]
     in_specs = [
         pl.BlockSpec((rows, 1), whole),
-        pl.BlockSpec((slots, BLOCK), lambda j, core: (0, j)),
-        pl.BlockSpec((rows, kv), whole),
-        pl.BlockSpec((1, depth, kv), deep),
-        pl.BlockSpec((1, depth, kv), deep),
-        pl.BlockSpec((1, BLOCK), column),
+        pl.BlockSpec((slots, BLOCK), lambda j: (0, j)),
+        pl.BlockSpec((rows, BLOCK), column),
         pl.BlockSpec((rows, 128), whole),
         pl.BlockSpec((rows, 128), whole),
     ]
     aliases = {}
     if packed is not None:
+        aliases = {len(operands): 0}
         operands.append(packed)
         in_specs.append(pl.BlockSpec(memory_space=pl.ANY))
-        aliases = {9: 0}
     return pl.pallas_call(
         first_pass_kernel,
-        grid_spec=pltpu.PrefetchScalarGridSpec(
-            num_scalar_prefetch=1,
-            grid=(part // BLOCK,),
-            in_specs=in_specs,
-            out_specs=[
-                pl.BlockSpec((rows, BLOCK), column),
-                pl.BlockSpec((rows, 128), whole),
-                pl.BlockSpec((rows, 128), whole),
-            ],
-            scratch_shapes=[pltpu.VMEM((rows, slots), jnp.bfloat16)],
-        ),
-        out_shape=(jax.ShapeDtypeStruct((rows, width), jnp.bfloat16), sums, sums),
+        grid=(part // BLOCK,),
+        in_specs=in_specs,
+        out_specs=[
+            pl.BlockSpec((rows, BLOCK), column),
+            pl.BlockSpec((rows, 128), whole),
+            pl.BlockSpec((rows, 128), whole),
+        ],
+        scratch_shapes=[pltpu.VMEM((rows, slots), jnp.bfloat16)],
+        out_shape=(jax.ShapeDtypeStruct((rows, total), jnp.bfloat16), sums, sums),
         input_output_aliases=aliases,
         cost_estimate=pl.CostEstimate(
-            flops=2 * rows * (slots + kv) * part,
-            bytes_accessed=2 * (slots + rows + kv) * part,
-            transcendentals=0,
+            flops=2 * rows * slots * part, bytes_accessed=(2 * slots + 6 * rows) * part, transcendentals=0
         ),
         compiler_params=pltpu.CompilerParams(vmem_limit_bytes=58 << 20),
         name="first_pass",
     )(*operands)
 
 
-def second_pass_kernel(
-    core_ref, packed_ref, key_ref, mine_ref, other_ref, gain_ref, square_ref, inner_ref, out_ref, inv, coef, *, width
+def last_pass_kernel(
+    select_ref, arrived_ref, scaled_ref, packed_ref, square_in, inner_in,
+    out_ref, gather, square, inner, inv, coef, kept, kept_scaled, *, early, late, width,
 ):
-    @pl.when(pl.program_id(0) == 0)
-    def _():
-        square = jnp.sum(square_ref[...], axis=1, keepdims=True) * (1.0 / width)
-        inner = jnp.sum(inner_ref[...], axis=1, keepdims=True) * (1.0 / width)
-        inverse = lax.rsqrt(square + norm_eps)
+    step = pl.program_id(0)
+
+    @pl.when(step == 0)
+    def _():
+        gather[...] = one_hot(select_ref[...], gather.shape[1])
+        square[...] = square_in[...]
+        inner[...] = inner_in[...]
+
+    @pl.when(step < late)
+    def _():
+        kept[step] = place_and_sum(gather, arrived_ref, scaled_ref, square, inner)
+        kept_scaled[step] = scaled_ref[...]
+
+    @pl.when(step == late)
+    def _():
+        inverse = lax.rsqrt(jnp.sum(square[...], axis=1, keepdims=True) * (1.0 / width) + norm_eps)
         inv[...] = inverse
-        coef[...] = inverse * inverse * inner
-
-    depth = mine_ref.shape[1]
-    core = core_ref[0]
-    for half, weight_ref in ((core, mine_ref), (1 - core, other_ref)):
-        cols = pl.ds(pl.multiple_of(half * depth, depth), depth)
-        scaled = delta_times_gain(key_ref[...], weight_ref[0], gain_ref[:, cols])
-        values = packed_ref[:, cols].astype(jnp.float32)
-        out_ref[:, cols] = (inv[...] * (scaled - values * coef[...])).astype(jnp.bfloat16)
-
-
-def second_pass(core, packed, key_grad, mine, other, gain, square, inner):
-    rows, kv = key_grad.shape
-    width = packed.shape[1]
-    depth = mine.shape[1]
-    whole = lambda j, core: (0, 0)
-    column = lambda j, core: (0, j)
-    deep = lambda j, core: (j, 0, 0)
+        coef[...] = inverse * inverse * (jnp.sum(inner[...], axis=1, keepdims=True) * (1.0 / width))
+
+    def finish(scaled, values):
+        out_ref[...] = (inv[...] * (scaled - values.astype(jnp.float32) * coef[...])).astype(jnp.bfloat16)
+
+    @pl.when((step >= late) & (step < late + early))
+    def _():
+        finish(scaled_ref[...], packed_ref[...])
+
+    @pl.when(step >= late + early)
+    def _():
+        i = step - (late + early)
+        finish(kept_scaled[i], kept[i])
+
+
+def last_pass(select, arrived, scaled, packed, square, inner):
+    rows, width = scaled.shape
+    slots = arrived.shape[0]
+    early, late = packed.shape[1] // BLOCK, arrived.shape[1] // BLOCK
+    whole = lambda j: (0, 0)
     return pl.pallas_call(
-        functools.partial(second_pass_kernel, width=width),
-        grid_spec=pltpu.PrefetchScalarGridSpec(
-            num_scalar_prefetch=1,
-            grid=(width // BLOCK,),
-            in_specs=[
-                pl.BlockSpec((rows, BLOCK), column),
-                pl.BlockSpec((rows, kv), whole),
-                pl.BlockSpec((1, depth, kv), deep),
-                pl.BlockSpec((1, depth, kv), deep),
-                pl.BlockSpec((1, BLOCK), column),
-                pl.BlockSpec((rows, 128), whole),
-                pl.BlockSpec((rows, 128), whole),
-            ],
-            out_specs=pl.BlockSpec((rows, BLOCK), column),
-            scratch_shapes=[pltpu.VMEM((rows, 1), jnp.float32), pltpu.VMEM((rows, 1), jnp.float32)],
-        ),
+        functools.partial(last_pass_kernel, early=early, late=late, width=width),
+        grid=(2 * late + early,),
+        in_specs=[
+            pl.BlockSpec((rows, 1), whole),
+            pl.BlockSpec((slots, BLOCK), lambda j: (0, jnp.minimum(j, late - 1))),
+            pl.BlockSpec(
+                (rows, BLOCK), lambda j: (0, jnp.where(j < late, early + j, jnp.minimum(j - late, early - 1)))
+            ),
+            pl.BlockSpec((rows, BLOCK), lambda j: (0, jnp.clip(j - late, 0, early - 1))),
+            pl.BlockSpec((rows, 128), whole),
+            pl.BlockSpec((rows, 128), whole),
+        ],
+        out_specs=pl.BlockSpec((rows, BLOCK), lambda j: (0, jnp.maximum(j - late, 0))),
+        scratch_shapes=[
+            pltpu.VMEM((rows, slots), jnp.bfloat16),
+            pltpu.VMEM((rows, 128), jnp.float32),
+            pltpu.VMEM((rows, 128), jnp.float32),
+            pltpu.VMEM((rows, 1), jnp.float32),
+            pltpu.VMEM((rows, 1), jnp.float32),
+            pltpu.VMEM((late, rows, BLOCK), jnp.bfloat16),
+            pltpu.VMEM((late, rows, BLOCK), jnp.float32),
+        ],
         out_shape=jax.ShapeDtypeStruct((rows, width), jnp.bfloat16),
         cost_estimate=pl.CostEstimate(
-            flops=2 * rows * kv * width, bytes_accessed=2 * (2 * rows + kv) * width, transcendentals=0
+            flops=2 * rows * slots * late * BLOCK, bytes_accessed=24 << 20, transcendentals=0
         ),
         compiler_params=pltpu.CompilerParams(vmem_limit_bytes=58 << 20),
-        name="second_pass",
-    )(core, packed, key_grad, mine, other, gain, square, inner)
+        name="last_pass",
+    )(select, arrived, scaled, packed, square, inner)
 
 
 CHUNKS = (3072, 5120)
@@ -342,7 +381,9 @@
     cosine, sine = rope_tables(position)
     key_grad, message = rope_and_spread(to_loader, cosine, sine, rotated_grad, CHUNKS[0])
     message = spread_rows(to_owner, layer_input, 0, CHUNKS[0], message)
-    outgoing = spread_rows(to_owner, layer_input, CHUNKS[0], CHUNKS[1])
+    outgoing = [
+        spread_rows(to_owner, layer_input, sum(CHUNKS[:i]), CHUNKS[i]) for i in range(1, len(CHUNKS))
+    ]
     message, other_z = lax.optimization_barrier((message, other_z))
     arrived = [exchange(message)]
 
@@ -354,10 +395,12 @@
     mine = mine.reshape(8, depth, kv)
     other = along_core(mine)
 
-    arrived[0], outgoing, later_input, mine, other = lax.optimization_barrier(
-        (arrived[0], outgoing, layer_input, mine, other)
+    first_in, outgoing[0], later_input, mine, other = lax.optimization_barrier(
+        (arrived[0], outgoing[0], layer_input, mine, other)
     )
-    arrived.append(exchange(outgoing))
+    arrived[0] = first_in
+    for rows_out in outgoing:
+        arrived.append(exchange(rows_out))
     key_back = arrived[0][:, CHUNKS[0] :]
     key_loader = lax.dot_general(
         (to_owner == row_ids[None, :]).astype(jnp.bfloat16),
@@ -387,21 +430,23 @@
         return total
 
     part = reduce(part.reshape(8, 4, 2 * rows, kv), 1, yy, along_y).astype(jnp.bfloat16)
-    part = part.reshape(2, 4, 2, rows, kv).transpose(0, 2, 1, 3, 4).reshape(4, 4, rows, kv)
-    part = reduce(part, 0, zz, along_z).astype(jnp.bfloat16)
-    weight_grad = reduce(part, 0, xx, along_x)
-
     core_id = jnp.reshape(core, (1,)).astype(jnp.int32)
     select = slot[:, None]
     square = jnp.zeros((tok_rows, 128), jnp.float32)
     inner = jnp.zeros((tok_rows, 128), jnp.float32)
+    scaled = scaled_delta(core_id, key_grad, mine, other, gain)
     packed, first = None, 0
-    for rows_in, part in zip(arrived, CHUNKS):
+    for rows_in, size in zip(arrived[:-1], CHUNKS[:-1]):
         packed, square, inner = first_pass(
-            core_id, select, rows_in, key_grad, mine, other, gain, square, inner, packed, first, part, width
+            select, rows_in, scaled, square, inner, packed, first, size, sum(CHUNKS[:-1])
         )
-        first += part
-    input_grad = second_pass(core_id, packed, key_grad, mine, other, gain, square, inner)
+        first += size
+    part, square, inner = lax.optimization_barrier((part, square, inner))
+    part = part.reshape(2, 4, 2, rows, kv).transpose(0, 2, 1, 3, 4).reshape(4, 4, rows, kv)
+    part = reduce(part, 0, zz, along_z).astype(jnp.bfloat16)
+    weight_grad = reduce(part, 0, xx, along_x)
+
+    input_grad = last_pass(select, arrived[-1], scaled, packed, square, inner)
     return (input_grad, weight_grad)
 
 

time: 318 us -> 305 us (0.959)
  waiting for transfers between devices: 159 us -> 140 us
  Pallas kernels: 58.2 us -> 66.3 us
  local copies, waits for them, and re-layouts: 23.2 us -> 18.7 us
    ppermute x6, waiting for transfers between devices: 82.6 us -> 62.2 us  [along_y(): lax.ppermute(v, AXES, perm(lambda zh, x, c, y, zl: (zh, x, c, y + n, zl)))]
    pallas_call x3, Pallas kernels: 36.6 us -> 44.5 us  [the longest x1 20.7 us: last_pass(): pl.pallas_call(functools.partial(last_pass_kernel, early=early, late=late...]
  transfers between devices with their start and end apart: 17 -> 17, of which waited for: 9 -> 9; matrix products, arithmetic and copies ran while one was open for 16% -> 15% of each run, Pallas kernels for 10% -> 15%
where the time goes in v3:
time: 305 us; the launch traced here: 303 us
  waiting for transfers between devices  140 us (46%)
  Pallas kernels  66.3 us (22%)
  starting transfers between devices  47.1 us (15%)
  local copies, waits for them, and re-layouts  18.7 us (6%)
  other arithmetic  18.3 us (6%)
  matrix products  11 us (4%)
    ppermute x6, waiting for transfers between devices, along_y(): lax.ppermute(v, AXES, perm(lambda zh, x, c, y, zl: (zh, x, c, y + n, zl)))  62.2 us
    ppermute x3, waiting for transfers between devices, along_z(): return lax.ppermute(v, AXES, perm(step))  35.3 us
    all_to_all x2, waiting for transfers between devices, exchange(): lax.all_to_all(blocks, 'dp', split_axis=0, concat_axis=0, tiled=True)  33.8 us
    pallas_call x1, Pallas kernels, last_pass(): pl.pallas_call(functools.partial(last_pass_kernel, early=early, late=late...  20.7 us
    pallas_call x2, Pallas kernels, spread_rows(): pl.pallas_call(spread_kernel, grid=(width // BLOCK,), in_specs=[pl.BlockS...  18.6 us
    ppermute x3, starting transfers between devices, along_x(): lax.ppermute(v, AXES, perm(lambda zh, x, c, y, zl: (zh, x + n, c, y, zl)))  16.1 us
    all_to_all x2, starting transfers between devices, exchange(): lax.all_to_all(blocks, 'dp', split_axis=0, concat_axis=0, tiled=True)  14.9 us
    pallas_call x1, Pallas kernels, scaled_delta(): pl.pallas_call(delta_kernel, grid_spec=pltpu.PrefetchScalarGridSpec(num_s...  13.1 us
  transfers between devices with their start and end apart: 17, of which 9 were waited for; matrix products, arithmetic and copies ran while one was open for 15% of the time, Pallas kernels for 15%

profile of v3, /device:TPU:1, one launch (start us, length us, event | category | flops | bytes accessed | tf_op | source)
XLA Modules:
  0.0 302.8 jit_solution(7782992711659097003)
XLA Ops:
  1.9 2.5 collective-permute-start
  11.6 3.3 %rope_and_spread.1 = (bf16[512,512]{1,0:T(8,128)(2,1)}, bf16[1024,3584]{1,0:T(8,128)(2,1)}) custom-call(s32[1024,1]{1,0:T(8,128)} %select_n.242.select_ref, f32[512,128]{1,0:T(8,128)} %get-tuple-element.49.cos_ref, f32[512,128]{1,0:T(8,128)} %get-tuple-element.48.sin_ref, bf16[512,512]{1,0:T(8,128)(2,1)} %rotated_ref.1), custom_call_target="tpu_custom_call" | custom-call | flops 536870912 | bytes 4194304 | tf_op jit(solution)/shard_map/rope_and_spread/pallas_call | solution.py:91
  14.9 7.4 %spread_rows.2 = bf16[1024,3584]{1,0:T(8,128)(2,1)} custom-call(s32[1024,1]{1,0:T(8,128)} %select_n.243.select_ref, bf16[512,8192]{1,0:T(8,128)(2,1)} %rows_ref.3, bf16[1024,3584]{1,0:T(8,128)(2,1)} %get-tuple-element.17.rest_0_), custom_call_target="tpu_custom_call", output_to_operand_aliasing={{}: (2, {})} | custom-call | flops 3221225472 | bytes 9437184 | tf_op jit(solution)/shard_map/spread_rows/pallas_call | solution.py:123
  22.3 8.3 %all-to-all-start = ((bf16[16,64,3584]{2,1,0:T(8,128)(2,1)}), bf16[16,64,3584]{2,1,0:T(8,128)(2,1)}, u32[]{:S(2)}, u32[]{:S(2)}) async-start(bf16[16,64,3584]{2,1,0:T(8,128)(2,1)} %bitcast.70), calls=%async_computation | async-start | bytes 14680064 | tf_op jit(solution)/shard_map/all_to_all | solution.py:375
  36.8 21.2 %collective-permute-done.1 = bf16[2,512,512]{2,1,0:T(8,128)(2,1)} collective-permute-done((bf16[2,512,512]{2,1,0:T(8,128)(2,1)}, bf16[2,512,512]{2,1,0:T(8,128)(2,1)}, u32[]{:S(2)}, u32[]{:S(2)}) %collective-permute-start.1) | collective-permute-done | bytes 1048608 | tf_op jit(solution)/shard_map/ppermute | solution.py:43
  60.7 20.9 %collective-permute-done.3 = bf16[2,512,512]{2,1,0:T(8,128)(2,1)} collective-permute-done((bf16[2,512,512]{2,1,0:T(8,128)(2,1)}, bf16[2,512,512]{2,1,0:T(8,128)(2,1)}, u32[]{:S(2)}, u32[]{:S(2)}) %collective-permute-start.3) | collective-permute-done | bytes 1048608 | tf_op jit(solution)/shard_map/ppermute | solution.py:43
  84.0 11.1 %spread_rows.3 = bf16[1024,5120]{1,0:T(8,128)(2,1)} custom-call(s32[1024,1]{1,0:T(8,128)} %select_n.243.select_ref, bf16[512,8192]{1,0:T(8,128)(2,1)} %rows_ref.3), custom_call_target="tpu_custom_call" | custom-call | flops 5368709120 | bytes 15728640 | tf_op jit(solution)/shard_map/spread_rows/pallas_call | solution.py:123
  95.2 33.8 %all-to-all-done = bf16[16,64,3584]{2,1,0:T(8,128)(2,1)} async-done(((bf16[16,64,3584]{2,1,0:T(8,128)(2,1)}), bf16[16,64,3584]{2,1,0:T(8,128)(2,1)}, u32[]{:S(2)}, u32[]{:S(2)}) %all-to-all-start) | async-done | bytes 7340064 | tf_op jit(solution)/shard_map/all_to_all | solution.py:375
  129.0 6.6 %all-to-all-start.1 = ((bf16[16,64,5120]{2,1,0:T(8,128)(2,1)}), bf16[16,64,5120]{2,1,0:T(8,128)(2,1)}, u32[]{:S(2)}, u32[]{:S(2)}) async-start(bf16[16,64,5120]{2,1,0:T(8,128)(2,1)} %bitcast.75), calls=%async_computation.1 | async-start | bytes 20971520 | tf_op jit(solution)/shard_map/all_to_all | solution.py:375
  135.7 5.1 %fusion = f32[512]{0:T(512)S(1)} fusion(bf16[512,8192]{1,0:T(8,128)(2,1)} %rows_ref.3), kind=kLoop, calls=%fused_computation.2 | loop fusion | flops 12582400 | bytes 8390656 | tf_op jit(solution)/shard_map/reduce_sum | solution.py:414
  140.8 11.0 %multiply_convert_fusion = bf16[8192,512]{1,0:T(8,128)(2,1)} fusion(bf16[512,8192]{1,0:T(8,128)(2,1)} %rows_ref.3, f32[8192]{0:T(1024)S(1)} %convert_element_type.90, f32[512]{0:T(512)S(1)} %add_rsqrt_fusion, bf16[1024,3584]{1,0:T(8,128)(2,1)} %bitcast.7.arrived_ref, s32[1024]{0:T(1024)S(1)} %select_n.217), kind=kOutput, calls=%fused_computation.5 | convolution fusion | flops 4857790464 | bytes 17864704 | tf_op jit(solution)/shard_map/dot_general | solution.py:418
  151.9 4.4 %dynamic-slice_bitcast_fusion = bf16[8,512,512]{2,1,0:T(8,128)(2,1)} fusion(bf16[8,2,512,512]{3,2,1,0:T(8,128)(2,1)} %bitcast.76, s32[]{:T(128)S(6)} %select_n.218), kind=kLoop, calls=%fused_computation.10 | loop fusion | bytes 8388612 | tf_op jit(solution)/shard_map/jit(dynamic_index_in_dim)/squeeze | solution.py:59
  156.4 7.3 %collective-permute-done.5 = bf16[8,512,512]{2,1,0:T(8,128)(2,1)} collective-permute-done((bf16[8,512,512]{2,1,0:T(8,128)(2,1)}, bf16[8,512,512]{2,1,0:T(8,128)(2,1)}, u32[]{:S(2)}, u32[]{:S(2)}) %collective-permute-start.5) | collective-permute-done | bytes 4194336 | tf_op jit(solution)/shard_map/ppermute | solution.py:35
  163.8 4.7 %fusion.4 = bf16[8,512,512]{2,1,0:T(8,128)(2,1)S(1)} fusion(bf16[8,512,512]{2,1,0:T(8,128)(2,1)} %collective-permute-done.5, bf16[8,2,512,512]{3,2,1,0:T(8,128)(2,1)} %bitcast.77, s32[]{:T(128)S(6)} %select_n.203), kind=kLoop, calls=%fused_computation.7 | loop fusion | flops 8388608 | bytes 12582916 | tf_op jit(solution)/shard_map/convert_element_type | solution.py:424
  168.5 2.0 copy-done.2
  177.3 13.1 %scaled_delta.1.scaled_ref = f32[512,8192]{1,0:T(8,128)} custom-call(s32[1]{0:T(128)} %bitcast.17.core_ref, bf16[512,512]{1,0:T(8,128)(2,1)} %get-tuple-element.21.key_ref, bf16[8,512,512]{2,1,0:T(8,128)(2,1)} %bitcast.74, bf16[8,512,512]{2,1,0:T(8,128)(2,1)} %collective-permute-done.4.other_ref, f32[1,8192]{1,0:T(1,128)} %bitcast.83), custom_call_target="tpu_custom_call" | custom-call | flops 4294967296 | bytes 25165824 | tf_op jit(solution)/shard_map/scaled_delta/pallas_call | solution.py:165
  191.2 10.6 %first_pass.1 = (bf16[512,3072]{1,0:T(8,128)(2,1)}, f32[512,128]{1,0:T(8,128)}, f32[512,128]{1,0:T(8,128)}) custom-call(s32[512,1]{1,0:T(8,128)} %iota_add_fusion.select_ref, bf16[1024,3584]{1,0:T(8,128)(2,1)} %bitcast.7.arrived_ref, f32[512,8192]{1,0:T(8,128)} %scaled_delta.1.scaled_ref, f32[512,128]{1,0:T(8,128)} %broadcast_2_square_in_inner_in.2.square_in.inner_in, ...), custom_call_target="tpu_custom_call" | custom-call | flops 3221225472 | bytes 15728640 | tf_op jit(solution)/shard_map/first_pass/pallas_call | solution.py:225
  201.8 20.1 %collective-permute-done.8 = bf16[8,128,512]{2,1,0:T(8,128)(2,1)} collective-permute-done((bf16[8,128,512]{2,1,0:T(8,128)(2,1)S(1)}, bf16[8,128,512]{2,1,0:T(8,128)(2,1)}, u32[]{:S(2)}, u32[]{:S(2)}) %collective-permute-start.8) | collective-permute-done | bytes 1048608 | tf_op jit(solution)/shard_map/ppermute | solution.py:43
  221.9 2.4 fusion.9
  228.1 26.4 %collective-permute-done.10 = bf16[4,64,512]{2,1,0:T(8,128)(2,1)S(1)} collective-permute-done((bf16[4,64,512]{2,1,0:T(8,128)(2,1)S(1)}, bf16[4,64,512]{2,1,0:T(8,128)(2,1)S(1)}, u32[]{:S(2)}, u32[]{:S(2)}) %collective-permute-start.10) | collective-permute-done | bytes 262176 | tf_op jit(solution)/shard_map/ppermute | solution.py:51
  254.5 3.0 collective-permute-done.11
  257.5 6.0 %collective-permute-done.9 = bf16[4,64,512]{2,1,0:T(8,128)(2,1)S(1)} collective-permute-done((bf16[4,64,512]{2,1,0:T(8,128)(2,1)S(1)}, bf16[4,64,512]{2,1,0:T(8,128)(2,1)S(1)}, u32[]{:S(2)}, u32[]{:S(2)}) %collective-permute-start.9) | collective-permute-done | bytes 262176 | tf_op jit(solution)/shard_map/ppermute | solution.py:51
  266.8 12.9 %collective-permute-start.14 = (bf16[64,512]{1,0:T(8,128)(2,1)S(1)}, bf16[64,512]{1,0:T(8,128)(2,1)S(1)}, u32[]{:S(2)}, u32[]{:S(2)}) collective-permute-start(bf16[64,512]{1,0:T(8,128)(2,1)S(1)} %get-tuple-element.46), channel_id=1, source_target_pairs={{0,32},{1,33},{2,34},{3,35},{4,36},{5,37},{6,38},{7,39},{8,40},{9,... | collective-permute-start | bytes 196616 | tf_op jit(solution)/shard_map/ppermute | solution.py:39
  282.1 20.7 %last_pass.1 = bf16[512,8192]{1,0:T(8,128)(2,1)} custom-call(s32[512,1]{1,0:T(8,128)} %iota_add_fusion.select_ref, bf16[1024,5120]{1,0:T(8,128)(2,1)} %bitcast.16.arrived_ref, f32[512,8192]{1,0:T(8,128)} %scaled_delta.1.scaled_ref, bf16[512,3072]{1,0:T(8,128)(2,1)} %get-tuple-element.25.packed_ref, f32[512,128]{1,0:T(8,128)} %get-tuple-element.29.square_in, ...), custom_call_target="tpu_custom_call" | custom-call | flops 5368709120 | bytes 25165824 | tf_op jit(solution)/shard_map/last_pass/pallas_call | solution.py:286
  (68 shorter events, 36.9 us)
Async XLA Ops:
  0.6 1.2 copy-start
  1.9 20.4 %collective-permute-start = (bf16[512,512]{1,0:T(8,128)(2,1)S(1)}, bf16[512,512]{1,0:T(8,128)(2,1)S(1)}, u32[]{:S(2)}, u32[]{:S(2)}) collective-permute-start(bf16[512,512]{1,0:T(8,128)(2,1)S(1)} %fusion.28), channel_id=1, source_target_pairs={{0,1},{1,0},{2,3},{3,2},{4,5},{5,4},{6,7},{7,6},{8,9},{9,8},{10,11... | collective-permute-start | bytes 1572872 | tf_op jit(solution)/shard_map/ppermute | solution.py:55
  22.3 106.6 %all-to-all-start = ((bf16[16,64,3584]{2,1,0:T(8,128)(2,1)}), bf16[16,64,3584]{2,1,0:T(8,128)(2,1)}, u32[]{:S(2)}, u32[]{:S(2)}) async-start(bf16[16,64,3584]{2,1,0:T(8,128)(2,1)} %bitcast.70), calls=%async_computation | async-start | bytes 14680064 | tf_op jit(solution)/shard_map/all_to_all | solution.py:375
  31.8 26.3 %collective-permute-start.1 = (bf16[2,512,512]{2,1,0:T(8,128)(2,1)}, bf16[2,512,512]{2,1,0:T(8,128)(2,1)}, u32[]{:S(2)}, u32[]{:S(2)}) collective-permute-start(bf16[2,512,512]{2,1,0:T(8,128)(2,1)} %maximum_select_fusion.1), channel_id=1, source_target_pairs={{0,2},{1,3},{2,4},{3,5},{4,6},{5,7},{6,0},{7,1},{8,10},{9,11},{10,... | collective-permute-start | bytes 3145736 | tf_op jit(solution)/shard_map/ppermute | solution.py:43
  33.1 26.3 %collective-permute-start.2 = (bf16[2,512,512]{2,1,0:T(8,128)(2,1)}, bf16[2,512,512]{2,1,0:T(8,128)(2,1)}, u32[]{:S(2)}, u32[]{:S(2)}) collective-permute-start(bf16[2,512,512]{2,1,0:T(8,128)(2,1)} %maximum_select_fusion.1), channel_id=1, source_target_pairs={{0,6},{1,7},{2,0},{3,1},{4,2},{5,3},{6,4},{7,5},{8,14},{9,15},{10,... | collective-permute-start | bytes 3145736 | tf_op jit(solution)/shard_map/ppermute | solution.py:43
  34.5 47.1 %collective-permute-start.3 = (bf16[2,512,512]{2,1,0:T(8,128)(2,1)}, bf16[2,512,512]{2,1,0:T(8,128)(2,1)}, u32[]{:S(2)}, u32[]{:S(2)}) collective-permute-start(bf16[2,512,512]{2,1,0:T(8,128)(2,1)} %maximum_select_fusion.1), channel_id=1, source_target_pairs={{0,4},{1,5},{2,6},{3,7},{4,0},{5,1},{6,2},{7,3},{8,12},{9,13},{10,... | collective-permute-start | bytes 3145736 | tf_op jit(solution)/shard_map/ppermute | solution.py:43
  83.0 12.2 %copy-start.3 = (bf16[4,2,512,512]{3,2,1,0:T(8,128)(2,1)}, bf16[4,2,512,512]{3,2,1,0:T(8,128)(2,1)S(1)}, u32[]{:S(2)}) copy-start(bf16[4,2,512,512]{3,2,1,0:T(8,128)(2,1)S(1)} %bitcast_dynamic-update-slice_fusion) | copy-start | bytes 12582916
  83.0 12.2 %collective-permute-start.4 = (bf16[8,512,512]{2,1,0:T(8,128)(2,1)S(1)}, bf16[8,512,512]{2,1,0:T(8,128)(2,1)}, u32[]{:S(2)}, u32[]{:S(2)}) collective-permute-start(bf16[8,512,512]{2,1,0:T(8,128)(2,1)S(1)} %bitcast.73), channel_id=1, source_target_pairs={{0,8},{1,9},{2,10},{3,11},{4,12},{5,13},{6,14},{7,15},{8,0},{9,1},... | collective-permute-start | bytes 12582920 | tf_op jit(solution)/shard_map/ppermute | solution.py:35
  129.0 6.7 %copy-start.5 = (bf16[8192]{0:T(1024)(128)(2,1)S(1)}, bf16[8192]{0:T(1024)(128)(2,1)}, u32[]{:S(2)}) copy-start(bf16[8192]{0:T(1024)(128)(2,1)} %param.11) | copy-start | bytes 49156
  129.0 153.1 %all-to-all-start.1 = ((bf16[16,64,5120]{2,1,0:T(8,128)(2,1)}), bf16[16,64,5120]{2,1,0:T(8,128)(2,1)}, u32[]{:S(2)}, u32[]{:S(2)}) async-start(bf16[16,64,5120]{2,1,0:T(8,128)(2,1)} %bitcast.75), calls=%async_computation.1 | async-start | bytes 20971520 | tf_op jit(solution)/shard_map/all_to_all | solution.py:375
  135.7 5.1 %copy-start.4 = (f32[8192]{0:T(1024)}, f32[8192]{0:T(1024)S(1)}, u32[]{:S(2)}) copy-start(f32[8192]{0:T(1024)S(1)} %convert_element_type.90) | copy-start | bytes 98308
  156.3 7.5 %collective-permute-start.5 = (bf16[8,512,512]{2,1,0:T(8,128)(2,1)}, bf16[8,512,512]{2,1,0:T(8,128)(2,1)}, u32[]{:S(2)}, u32[]{:S(2)}) collective-permute-start(bf16[8,512,512]{2,1,0:T(8,128)(2,1)} %dynamic-slice_bitcast_fusion), channel_id=1, source_target_pairs={{0,8},{1,9},{2,10},{3,11},{4,12},{5,13},{6,14},{7,15},{8,0},{9,1},... | collective-permute-start | bytes 12582920 | tf_op jit(solution)/shard_map/ppermute | solution.py:35
  168.5 2.0 copy-start.2
  172.1 29.7 %collective-permute-start.6 = (bf16[8,128,512]{2,1,0:T(8,128)(2,1)}, bf16[8,128,512]{2,1,0:T(8,128)(2,1)S(1)}, u32[]{:S(2)}, u32[]{:S(2)}) collective-permute-start(bf16[8,128,512]{2,1,0:T(8,128)(2,1)} %get-tuple-element.39), channel_id=1, source_target_pairs={{0,2},{1,3},{2,4},{3,5},{4,6},{5,7},{6,0},{7,1},{8,10},{9,11},{10,... | collective-permute-start | bytes 3145736 | tf_op jit(solution)/shard_map/ppermute | solution.py:43
  173.3 28.5 %collective-permute-start.7 = (bf16[8,128,512]{2,1,0:T(8,128)(2,1)}, bf16[8,128,512]{2,1,0:T(8,128)(2,1)}, u32[]{:S(2)}, u32[]{:S(2)}) collective-permute-start(bf16[8,128,512]{2,1,0:T(8,128)(2,1)} %get-tuple-element.41), channel_id=1, source_target_pairs={{0,6},{1,7},{2,0},{3,1},{4,2},{5,3},{6,4},{7,5},{8,14},{9,15},{10,... | collective-permute-start | bytes 3145736 | tf_op jit(solution)/shard_map/ppermute | solution.py:43
  174.8 47.1 %collective-permute-start.8 = (bf16[8,128,512]{2,1,0:T(8,128)(2,1)S(1)}, bf16[8,128,512]{2,1,0:T(8,128)(2,1)}, u32[]{:S(2)}, u32[]{:S(2)}) collective-permute-start(bf16[8,128,512]{2,1,0:T(8,128)(2,1)S(1)} %get-tuple-element.40), channel_id=1, source_target_pairs={{0,4},{1,5},{2,6},{3,7},{4,0},{5,1},{6,2},{7,3},{8,12},{9,13},{10,... | collective-permute-start | bytes 3145736 | tf_op jit(solution)/shard_map/ppermute | solution.py:43
  224.5 30.0 %collective-permute-start.10 = (bf16[4,64,512]{2,1,0:T(8,128)(2,1)S(1)}, bf16[4,64,512]{2,1,0:T(8,128)(2,1)S(1)}, u32[]{:S(2)}, u32[]{:S(2)}) collective-permute-start(bf16[4,64,512]{2,1,0:T(8,128)(2,1)S(1)} %get-tuple-element.44), channel_id=1, source_target_pairs={{0,65},{1,0},{2,67},{3,2},{4,69},{5,4},{6,71},{7,6},{8,73},{9,8},{... | collective-permute-start | bytes 786440 | tf_op jit(solution)/shard_map/ppermute | solution.py:51
  226.2 31.3 %collective-permute-start.11 = (bf16[4,64,512]{2,1,0:T(8,128)(2,1)S(1)}, bf16[4,64,512]{2,1,0:T(8,128)(2,1)S(1)}, u32[]{:S(2)}, u32[]{:S(2)}) collective-permute-start(bf16[4,64,512]{2,1,0:T(8,128)(2,1)S(1)} %get-tuple-element.43), channel_id=1, source_target_pairs={{0,64},{1,65},{2,66},{3,67},{4,68},{5,69},{6,70},{7,71},{8,72},{9,... | collective-permute-start | bytes 786440 | tf_op jit(solution)/shard_map/ppermute | solution.py:51
  227.4 36.1 %collective-permute-start.9 = (bf16[4,64,512]{2,1,0:T(8,128)(2,1)S(1)}, bf16[4,64,512]{2,1,0:T(8,128)(2,1)S(1)}, u32[]{:S(2)}, u32[]{:S(2)}) collective-permute-start(bf16[4,64,512]{2,1,0:T(8,128)(2,1)S(1)} %get-tuple-element.42), channel_id=1, source_target_pairs={{0,1},{1,64},{2,3},{3,66},{4,5},{5,68},{6,7},{7,70},{8,9},{9,72},{... | collective-permute-start | bytes 786440 | tf_op jit(solution)/shard_map/ppermute | solution.py:51
  263.6 16.1 %collective-permute-start.12 = (bf16[64,512]{1,0:T(8,128)(2,1)S(1)}, bf16[64,512]{1,0:T(8,128)(2,1)S(1)}, u32[]{:S(2)}, u32[]{:S(2)}) collective-permute-start(bf16[64,512]{1,0:T(8,128)(2,1)S(1)} %get-tuple-element.45), channel_id=1, source_target_pairs={{0,16},{1,17},{2,18},{3,19},{4,20},{5,21},{6,22},{7,23},{8,24},{9,... | collective-permute-start | bytes 196616 | tf_op jit(solution)/shard_map/ppermute | solution.py:39
  265.1 14.7 %collective-permute-start.13 = (bf16[64,512]{1,0:T(8,128)(2,1)S(1)}, bf16[64,512]{1,0:T(8,128)(2,1)S(1)}, u32[]{:S(2)}, u32[]{:S(2)}) collective-permute-start(bf16[64,512]{1,0:T(8,128)(2,1)S(1)} %get-tuple-element.47), channel_id=1, source_target_pairs={{0,48},{1,49},{2,50},{3,51},{4,52},{5,53},{6,54},{7,55},{8,56},{9,... | collective-permute-start | bytes 196616 | tf_op jit(solution)/shard_map/ppermute | solution.py:39
  266.8 14.6 %collective-permute-start.14 = (bf16[64,512]{1,0:T(8,128)(2,1)S(1)}, bf16[64,512]{1,0:T(8,128)(2,1)S(1)}, u32[]{:S(2)}, u32[]{:S(2)}) collective-permute-start(bf16[64,512]{1,0:T(8,128)(2,1)S(1)} %get-tuple-element.46), channel_id=1, source_target_pairs={{0,32},{1,33},{2,34},{3,35},{4,36},{5,37},{6,38},{7,39},{8,40},{9,... | collective-permute-start | bytes 196616 | tf_op jit(solution)/shard_map/ppermute | solution.py:39
  282.1 20.7 %copy-start.1 = (bf16[1024,512]{1,0:T(8,128)(2,1)S(1)}, bf16[1024,512]{1,0:T(8,128)(2,1)}, u32[]{:S(2)}) copy-start(bf16[1024,512]{1,0:T(8,128)(2,1)} %param.12) | copy-start | bytes 3145732

commit v4 on v3

--- a/solution.py
+++ b/solution.py
@@ -155,7 +155,7 @@
         delta = lax.dot_general(
             key_ref[...], weight_ref[0], (((1,), (1,)), ((), ())), preferred_element_type=jnp.float32
         )
-        out_ref[:, cols] = delta * gain_ref[:, cols]
+        out_ref[:, cols] = (delta * gain_ref[:, cols]).astype(jnp.bfloat16)
 
 
 def scaled_delta(core, key_grad, mine, other, gain):
@@ -175,9 +175,9 @@
             ],
             out_specs=pl.BlockSpec((rows, 2 * depth), lambda j, core: (0, j)),
         ),
-        out_shape=jax.ShapeDtypeStruct((rows, width), jnp.float32),
+        out_shape=jax.ShapeDtypeStruct((rows, width), jnp.bfloat16),
         cost_estimate=pl.CostEstimate(
-            flops=2 * rows * kv * width, bytes_accessed=(4 * rows + 2 * kv) * width, transcendentals=0
+            flops=2 * rows * kv * width, bytes_accessed=2 * (rows + kv) * width, transcendentals=0
         ),
         compiler_params=pltpu.CompilerParams(vmem_limit_bytes=58 << 20),
         name="scaled_delta",
@@ -187,7 +187,7 @@
 def place_and_sum(gather, arrived_ref, scaled_ref, square_ref, inner_ref):
     values = jnp.dot(gather[...], arrived_ref[...], preferred_element_type=jnp.float32)
     square_ref[...] += lane_sums(values * values)
-    inner_ref[...] += lane_sums(scaled_ref[...] * values)
+    inner_ref[...] += lane_sums(scaled_ref[...].astype(jnp.float32) * values)
     return values.astype(jnp.bfloat16)
 
 
@@ -266,7 +266,9 @@
         coef[...] = inverse * inverse * (jnp.sum(inner[...], axis=1, keepdims=True) * (1.0 / width))
 
     def finish(scaled, values):
-        out_ref[...] = (inv[...] * (scaled - values.astype(jnp.float32) * coef[...])).astype(jnp.bfloat16)
+        out_ref[...] = (
+            inv[...] * (scaled.astype(jnp.float32) - values.astype(jnp.float32) * coef[...])
+        ).astype(jnp.bfloat16)
 
     @pl.when((step >= late) & (step < late + early))
     def _():
@@ -304,7 +306,7 @@
             pltpu.VMEM((rows, 1), jnp.float32),
             pltpu.VMEM((rows, 1), jnp.float32),
             pltpu.VMEM((late, rows, BLOCK), jnp.bfloat16),
-            pltpu.VMEM((late, rows, BLOCK), jnp.float32),
+            pltpu.VMEM((late, rows, BLOCK), jnp.bfloat16),
         ],
         out_shape=jax.ShapeDtypeStruct((rows, width), jnp.bfloat16),
         cost_estimate=pl.CostEstimate(
@@ -444,9 +446,14 @@
     part, square, inner = lax.optimization_barrier((part, square, inner))
     part = part.reshape(2, 4, 2, rows, kv).transpose(0, 2, 1, 3, 4).reshape(4, 4, rows, kv)
     part = reduce(part, 0, zz, along_z).astype(jnp.bfloat16)
-    weight_grad = reduce(part, 0, xx, along_x)
+    kept = pick(part, xx)
+    pieces = [along_x(pick(part, (xx + n) % 4), n) for n in (1, 3, 2)]
 
     input_grad = last_pass(select, arrived[-1], scaled, packed, square, inner)
+    input_grad, kept, pieces = lax.optimization_barrier((input_grad, kept, pieces))
+    weight_grad = kept.astype(jnp.float32)
+    for piece in pieces:
+        weight_grad = weight_grad + piece.astype(jnp.float32)
     return (input_grad, weight_grad)
 
 

time: 305 us -> 300 us (0.984)
  Pallas kernels: 66.3 us -> 61.6 us
  transfers between devices with their start and end apart: 17 -> 17, of which waited for: 9 -> 9; matrix products, arithmetic and copies ran while one was open for 15% -> 15% of each run, Pallas kernels for 15% -> 21%
where the time goes in v4:
time: 300 us; the launch traced here: 299 us
  waiting for transfers between devices  141 us (47%)
  Pallas kernels  61.6 us (21%)
  starting transfers between devices  47.7 us (16%)
  local copies, waits for them, and re-layouts  18.8 us (6%)
  other arithmetic  18.3 us (6%)
  matrix products  11 us (4%)
    ppermute x6, waiting for transfers between devices, along_y(): lax.ppermute(v, AXES, perm(lambda zh, x, c, y, zl: (zh, x, c, y + n, zl)))  64.7 us
    ppermute x3, waiting for transfers between devices, along_z(): return lax.ppermute(v, AXES, perm(step))  34.9 us
    all_to_all x2, waiting for transfers between devices, exchange(): lax.all_to_all(blocks, 'dp', split_axis=0, concat_axis=0, tiled=True)  33.8 us
    pallas_call x1, Pallas kernels, last_pass(): pl.pallas_call(functools.partial(last_pass_kernel, early=early, late=late...  19 us
    pallas_call x2, Pallas kernels, spread_rows(): pl.pallas_call(spread_kernel, grid=(width // BLOCK,), in_specs=[pl.BlockS...  18.6 us
    ppermute x3, starting transfers between devices, along_x(): lax.ppermute(v, AXES, perm(lambda zh, x, c, y, zl: (zh, x + n, c, y, zl)))  15.9 us
    all_to_all x2, starting transfers between devices, exchange(): lax.all_to_all(blocks, 'dp', split_axis=0, concat_axis=0, tiled=True)  14.9 us
    pallas_call x1, Pallas kernels, scaled_delta(): pl.pallas_call(delta_kernel, grid_spec=pltpu.PrefetchScalarGridSpec(num_s...  11.4 us
  transfers between devices with their start and end apart: 17, of which 9 were waited for; matrix products, arithmetic and copies ran while one was open for 15% of the time, Pallas kernels for 21%

profile of v4, /device:TPU:1, one launch (start us, length us, event | category | flops | bytes accessed | tf_op | source)
XLA Modules:
  0.0 299.2 jit_solution(6566526686588614082)
XLA Ops:
  1.9 2.5 collective-permute-start
  11.6 3.3 %rope_and_spread.1 = (bf16[512,512]{1,0:T(8,128)(2,1)}, bf16[1024,3584]{1,0:T(8,128)(2,1)}) custom-call(s32[1024,1]{1,0:T(8,128)} %select_n.242.select_ref, f32[512,128]{1,0:T(8,128)} %get-tuple-element.60.cos_ref, f32[512,128]{1,0:T(8,128)} %get-tuple-element.59.sin_ref, bf16[512,512]{1,0:T(8,128)(2,1)} %rotated_ref.1), custom_call_target="tpu_custom_call" | custom-call | flops 536870912 | bytes 4194304 | tf_op jit(solution)/shard_map/rope_and_spread/pallas_call | solution.py:91
  14.9 7.4 %spread_rows.2 = bf16[1024,3584]{1,0:T(8,128)(2,1)} custom-call(s32[1024,1]{1,0:T(8,128)} %select_n.243.select_ref, bf16[512,8192]{1,0:T(8,128)(2,1)} %rows_ref.3, bf16[1024,3584]{1,0:T(8,128)(2,1)} %get-tuple-element.22.rest_0_), custom_call_target="tpu_custom_call", output_to_operand_aliasing={{}: (2, {})} | custom-call | flops 3221225472 | bytes 9437184 | tf_op jit(solution)/shard_map/spread_rows/pallas_call | solution.py:123
  22.3 8.3 %all-to-all-start = ((bf16[16,64,3584]{2,1,0:T(8,128)(2,1)}), bf16[16,64,3584]{2,1,0:T(8,128)(2,1)}, u32[]{:S(2)}, u32[]{:S(2)}) async-start(bf16[16,64,3584]{2,1,0:T(8,128)(2,1)} %bitcast.67), calls=%async_computation | async-start | bytes 14680064 | tf_op jit(solution)/shard_map/all_to_all | solution.py:377
  36.8 21.2 %collective-permute-done.1 = bf16[2,512,512]{2,1,0:T(8,128)(2,1)} collective-permute-done((bf16[2,512,512]{2,1,0:T(8,128)(2,1)}, bf16[2,512,512]{2,1,0:T(8,128)(2,1)}, u32[]{:S(2)}, u32[]{:S(2)}) %collective-permute-start.1) | collective-permute-done | bytes 1048608 | tf_op jit(solution)/shard_map/ppermute | solution.py:43
  60.7 20.9 %collective-permute-done.3 = bf16[2,512,512]{2,1,0:T(8,128)(2,1)} collective-permute-done((bf16[2,512,512]{2,1,0:T(8,128)(2,1)}, bf16[2,512,512]{2,1,0:T(8,128)(2,1)}, u32[]{:S(2)}, u32[]{:S(2)}) %collective-permute-start.3) | collective-permute-done | bytes 1048608 | tf_op jit(solution)/shard_map/ppermute | solution.py:43
  84.0 11.1 %spread_rows.3 = bf16[1024,5120]{1,0:T(8,128)(2,1)} custom-call(s32[1024,1]{1,0:T(8,128)} %select_n.243.select_ref, bf16[512,8192]{1,0:T(8,128)(2,1)} %rows_ref.3), custom_call_target="tpu_custom_call" | custom-call | flops 5368709120 | bytes 15728640 | tf_op jit(solution)/shard_map/spread_rows/pallas_call | solution.py:123
  95.1 33.8 %all-to-all-done = bf16[16,64,3584]{2,1,0:T(8,128)(2,1)} async-done(((bf16[16,64,3584]{2,1,0:T(8,128)(2,1)}), bf16[16,64,3584]{2,1,0:T(8,128)(2,1)}, u32[]{:S(2)}, u32[]{:S(2)}) %all-to-all-start) | async-done | bytes 7340064 | tf_op jit(solution)/shard_map/all_to_all | solution.py:377
  129.0 6.6 %all-to-all-start.1 = ((bf16[16,64,5120]{2,1,0:T(8,128)(2,1)}), bf16[16,64,5120]{2,1,0:T(8,128)(2,1)}, u32[]{:S(2)}, u32[]{:S(2)}) async-start(bf16[16,64,5120]{2,1,0:T(8,128)(2,1)} %bitcast.72), calls=%async_computation.1 | async-start | bytes 20971520 | tf_op jit(solution)/shard_map/all_to_all | solution.py:377
  135.7 5.1 %fusion = f32[512]{0:T(512)S(1)} fusion(bf16[512,8192]{1,0:T(8,128)(2,1)} %rows_ref.3), kind=kLoop, calls=%fused_computation.2 | loop fusion | flops 12582400 | bytes 8390656 | tf_op jit(solution)/shard_map/reduce_sum | solution.py:416
  140.8 11.0 %multiply_convert_fusion = bf16[8192,512]{1,0:T(8,128)(2,1)} fusion(bf16[512,8192]{1,0:T(8,128)(2,1)} %rows_ref.3, f32[8192]{0:T(1024)S(1)} %convert_element_type.87, f32[512]{0:T(512)S(1)} %add_rsqrt_fusion, bf16[1024,3584]{1,0:T(8,128)(2,1)} %bitcast.7.arrived_ref, s32[1024]{0:T(1024)S(1)} %select_n.217), kind=kOutput, calls=%fused_computation.5 | convolution fusion | flops 4857790464 | bytes 17864704 | tf_op jit(solution)/shard_map/dot_general | solution.py:420
  151.8 4.4 %dynamic-slice_bitcast_fusion = bf16[8,512,512]{2,1,0:T(8,128)(2,1)} fusion(bf16[8,2,512,512]{3,2,1,0:T(8,128)(2,1)} %bitcast.73, s32[]{:T(128)S(6)} %select_n.218), kind=kLoop, calls=%fused_computation.10 | loop fusion | bytes 8388612 | tf_op jit(solution)/shard_map/jit(dynamic_index_in_dim)/squeeze | solution.py:59
  156.4 7.3 %collective-permute-done.5 = bf16[8,512,512]{2,1,0:T(8,128)(2,1)} collective-permute-done((bf16[8,512,512]{2,1,0:T(8,128)(2,1)}, bf16[8,512,512]{2,1,0:T(8,128)(2,1)}, u32[]{:S(2)}, u32[]{:S(2)}) %collective-permute-start.5) | collective-permute-done | bytes 4194336 | tf_op jit(solution)/shard_map/ppermute | solution.py:35
  163.8 4.7 %fusion.4 = bf16[8,512,512]{2,1,0:T(8,128)(2,1)S(1)} fusion(bf16[8,512,512]{2,1,0:T(8,128)(2,1)} %collective-permute-done.5, bf16[8,2,512,512]{3,2,1,0:T(8,128)(2,1)} %bitcast.74, s32[]{:T(128)S(6)} %select_n.203), kind=kLoop, calls=%fused_computation.7 | loop fusion | flops 8388608 | bytes 12582916 | tf_op jit(solution)/shard_map/convert_element_type | solution.py:426
  172.1 2.9 collective-permute-start.8
  177.3 11.4 %scaled_delta.1.scaled_ref = bf16[512,8192]{1,0:T(8,128)(2,1)} custom-call(s32[1]{0:T(128)} %bitcast.17.core_ref, bf16[512,512]{1,0:T(8,128)(2,1)} %get-tuple-element.26.key_ref, bf16[8,512,512]{2,1,0:T(8,128)(2,1)} %bitcast.69, bf16[8,512,512]{2,1,0:T(8,128)(2,1)} %collective-permute-done.4.other_ref, f32[1,8192]{1,0:T(1,128)} %bitcast.80), custom_call_target="tpu_custom_call" | custom-call | flops 4294967296 | bytes 16777216 | tf_op jit(solution)/shard_map/scaled_delta/pallas_call | solution.py:165
  189.5 9.4 %first_pass.1 = (bf16[512,3072]{1,0:T(8,128)(2,1)}, f32[512,128]{1,0:T(8,128)}, f32[512,128]{1,0:T(8,128)}) custom-call(s32[512,1]{1,0:T(8,128)} %iota_add_fusion.select_ref, bf16[1024,3584]{1,0:T(8,128)(2,1)} %bitcast.7.arrived_ref, bf16[512,8192]{1,0:T(8,128)(2,1)} %scaled_delta.1.scaled_ref, f32[512,128]{1,0:T(8,128)} %broadcast_2_square_in_inner_in.2.square_in.inner_in, ...), custom_call_target="tpu_custom_call" | custom-call | flops 3221225472 | bytes 15728640 | tf_op jit(solution)/shard_map/first_pass/pallas_call | solution.py:225
  198.9 22.5 %collective-permute-done.7 = bf16[8,128,512]{2,1,0:T(8,128)(2,1)} collective-permute-done((bf16[8,128,512]{2,1,0:T(8,128)(2,1)}, bf16[8,128,512]{2,1,0:T(8,128)(2,1)}, u32[]{:S(2)}, u32[]{:S(2)}) %collective-permute-start.7) | collective-permute-done | bytes 1048608 | tf_op jit(solution)/shard_map/ppermute | solution.py:43
  224.1 3.0 collective-permute-start.11
  228.5 29.0 %collective-permute-done.11 = bf16[4,64,512]{2,1,0:T(8,128)(2,1)S(1)} collective-permute-done((bf16[4,64,512]{2,1,0:T(8,128)(2,1)S(1)}, bf16[4,64,512]{2,1,0:T(8,128)(2,1)S(1)}, u32[]{:S(2)}, u32[]{:S(2)}) %collective-permute-start.11) | collective-permute-done | bytes 262176 | tf_op jit(solution)/shard_map/ppermute | solution.py:51
  257.5 2.5 collective-permute-done.10
  260.0 3.4 %collective-permute-done.9 = bf16[4,64,512]{2,1,0:T(8,128)(2,1)S(1)} collective-permute-done((bf16[4,64,512]{2,1,0:T(8,128)(2,1)S(1)}, bf16[4,64,512]{2,1,0:T(8,128)(2,1)S(1)}, u32[]{:S(2)}, u32[]{:S(2)}) %collective-permute-start.9) | collective-permute-done | bytes 262176 | tf_op jit(solution)/shard_map/ppermute | solution.py:51
  266.6 12.9 %collective-permute-start.14 = (bf16[64,512]{1,0:T(8,128)(2,1)S(1)}, bf16[64,512]{1,0:T(8,128)(2,1)S(1)}, u32[]{:S(2)}, u32[]{:S(2)}) collective-permute-start(bf16[64,512]{1,0:T(8,128)(2,1)S(1)} %get-tuple-element.55), channel_id=1, source_target_pairs={{0,32},{1,33},{2,34},{3,35},{4,36},{5,37},{6,38},{7,39},{8,40},{9,... | collective-permute-start | bytes 196616 | tf_op jit(solution)/shard_map/ppermute | solution.py:39
  279.5 19.0 %last_pass.1 = bf16[512,8192]{1,0:T(8,128)(2,1)} custom-call(s32[512,1]{1,0:T(8,128)} %iota_add_fusion.select_ref, bf16[1024,5120]{1,0:T(8,128)(2,1)} %bitcast.16.arrived_ref, bf16[512,8192]{1,0:T(8,128)(2,1)} %scaled_delta.1.scaled_ref, bf16[512,3072]{1,0:T(8,128)(2,1)} %get-tuple-element.30.packed_ref, f32[512,128]{1,0:T(8,128)} %get-tuple-element.34.square_in, ...), custom_call_target="tpu_custom_call" | custom-call | flops 5368709120 | bytes 25165824 | tf_op jit(solution)/shard_map/last_pass/pallas_call | solution.py:288
  (68 shorter events, 34.5 us)
Async XLA Ops:
  0.6 1.2 copy-start
  1.9 20.4 %collective-permute-start = (bf16[512,512]{1,0:T(8,128)(2,1)S(1)}, bf16[512,512]{1,0:T(8,128)(2,1)S(1)}, u32[]{:S(2)}, u32[]{:S(2)}) collective-permute-start(bf16[512,512]{1,0:T(8,128)(2,1)S(1)} %fusion.26), channel_id=1, source_target_pairs={{0,1},{1,0},{2,3},{3,2},{4,5},{5,4},{6,7},{7,6},{8,9},{9,8},{10,11... | collective-permute-start | bytes 1572872 | tf_op jit(solution)/shard_map/ppermute | solution.py:55
  22.3 106.6 %all-to-all-start = ((bf16[16,64,3584]{2,1,0:T(8,128)(2,1)}), bf16[16,64,3584]{2,1,0:T(8,128)(2,1)}, u32[]{:S(2)}, u32[]{:S(2)}) async-start(bf16[16,64,3584]{2,1,0:T(8,128)(2,1)} %bitcast.67), calls=%async_computation | async-start | bytes 14680064 | tf_op jit(solution)/shard_map/all_to_all | solution.py:377
  31.8 26.3 %collective-permute-start.1 = (bf16[2,512,512]{2,1,0:T(8,128)(2,1)}, bf16[2,512,512]{2,1,0:T(8,128)(2,1)}, u32[]{:S(2)}, u32[]{:S(2)}) collective-permute-start(bf16[2,512,512]{2,1,0:T(8,128)(2,1)} %maximum_select_fusion.1), channel_id=1, source_target_pairs={{0,2},{1,3},{2,4},{3,5},{4,6},{5,7},{6,0},{7,1},{8,10},{9,11},{10,... | collective-permute-start | bytes 3145736 | tf_op jit(solution)/shard_map/ppermute | solution.py:43
  33.1 26.3 %collective-permute-start.2 = (bf16[2,512,512]{2,1,0:T(8,128)(2,1)}, bf16[2,512,512]{2,1,0:T(8,128)(2,1)}, u32[]{:S(2)}, u32[]{:S(2)}) collective-permute-start(bf16[2,512,512]{2,1,0:T(8,128)(2,1)} %maximum_select_fusion.1), channel_id=1, source_target_pairs={{0,6},{1,7},{2,0},{3,1},{4,2},{5,3},{6,4},{7,5},{8,14},{9,15},{10,... | collective-permute-start | bytes 3145736 | tf_op jit(solution)/shard_map/ppermute | solution.py:43
  34.5 47.1 %collective-permute-start.3 = (bf16[2,512,512]{2,1,0:T(8,128)(2,1)}, bf16[2,512,512]{2,1,0:T(8,128)(2,1)}, u32[]{:S(2)}, u32[]{:S(2)}) collective-permute-start(bf16[2,512,512]{2,1,0:T(8,128)(2,1)} %maximum_select_fusion.1), channel_id=1, source_target_pairs={{0,4},{1,5},{2,6},{3,7},{4,0},{5,1},{6,2},{7,3},{8,12},{9,13},{10,... | collective-permute-start | bytes 3145736 | tf_op jit(solution)/shard_map/ppermute | solution.py:43
  82.9 12.2 %copy-start.2 = (bf16[4,2,512,512]{3,2,1,0:T(8,128)(2,1)}, bf16[4,2,512,512]{3,2,1,0:T(8,128)(2,1)S(1)}, u32[]{:S(2)}) copy-start(bf16[4,2,512,512]{3,2,1,0:T(8,128)(2,1)S(1)} %bitcast_dynamic-update-slice_fusion) | copy-start | bytes 12582916
  83.0 12.2 %collective-permute-start.4 = (bf16[8,512,512]{2,1,0:T(8,128)(2,1)S(1)}, bf16[8,512,512]{2,1,0:T(8,128)(2,1)}, u32[]{:S(2)}, u32[]{:S(2)}) collective-permute-start(bf16[8,512,512]{2,1,0:T(8,128)(2,1)S(1)} %bitcast.68), channel_id=1, source_target_pairs={{0,8},{1,9},{2,10},{3,11},{4,12},{5,13},{6,14},{7,15},{8,0},{9,1},... | collective-permute-start | bytes 12582920 | tf_op jit(solution)/shard_map/ppermute | solution.py:35
  129.0 6.7 %copy-start.5 = (bf16[8192]{0:T(1024)(128)(2,1)S(1)}, bf16[8192]{0:T(1024)(128)(2,1)}, u32[]{:S(2)}) copy-start(bf16[8192]{0:T(1024)(128)(2,1)} %param.11) | copy-start | bytes 49156
  129.0 150.5 %all-to-all-start.1 = ((bf16[16,64,5120]{2,1,0:T(8,128)(2,1)}), bf16[16,64,5120]{2,1,0:T(8,128)(2,1)}, u32[]{:S(2)}, u32[]{:S(2)}) async-start(bf16[16,64,5120]{2,1,0:T(8,128)(2,1)} %bitcast.72), calls=%async_computation.1 | async-start | bytes 20971520 | tf_op jit(solution)/shard_map/all_to_all | solution.py:377
  135.7 5.1 %copy-start.4 = (f32[8192]{0:T(1024)}, f32[8192]{0:T(1024)S(1)}, u32[]{:S(2)}) copy-start(f32[8192]{0:T(1024)S(1)} %convert_element_type.87) | copy-start | bytes 98308
  156.3 7.5 %collective-permute-start.5 = (bf16[8,512,512]{2,1,0:T(8,128)(2,1)}, bf16[8,512,512]{2,1,0:T(8,128)(2,1)}, u32[]{:S(2)}, u32[]{:S(2)}) collective-permute-start(bf16[8,512,512]{2,1,0:T(8,128)(2,1)} %dynamic-slice_bitcast_fusion), channel_id=1, source_target_pairs={{0,8},{1,9},{2,10},{3,11},{4,12},{5,13},{6,14},{7,15},{8,0},{9,1},... | collective-permute-start | bytes 12582920 | tf_op jit(solution)/shard_map/ppermute | solution.py:35
  168.5 2.0 copy-start.3
  172.1 26.8 %collective-permute-start.8 = (bf16[8,128,512]{2,1,0:T(8,128)(2,1)}, bf16[8,128,512]{2,1,0:T(8,128)(2,1)S(1)}, u32[]{:S(2)}, u32[]{:S(2)}) collective-permute-start(bf16[8,128,512]{2,1,0:T(8,128)(2,1)} %get-tuple-element.50), channel_id=1, source_target_pairs={{0,4},{1,5},{2,6},{3,7},{4,0},{5,1},{6,2},{7,3},{8,12},{9,13},{10,... | collective-permute-start | bytes 3145736 | tf_op jit(solution)/shard_map/ppermute | solution.py:43
  175.0 46.4 %collective-permute-start.7 = (bf16[8,128,512]{2,1,0:T(8,128)(2,1)}, bf16[8,128,512]{2,1,0:T(8,128)(2,1)}, u32[]{:S(2)}, u32[]{:S(2)}) collective-permute-start(bf16[8,128,512]{2,1,0:T(8,128)(2,1)} %get-tuple-element.51), channel_id=1, source_target_pairs={{0,6},{1,7},{2,0},{3,1},{4,2},{5,3},{6,4},{7,5},{8,14},{9,15},{10,... | collective-permute-start | bytes 3145736 | tf_op jit(solution)/shard_map/ppermute | solution.py:43
  175.8 45.7 %collective-permute-start.6 = (bf16[8,128,512]{2,1,0:T(8,128)(2,1)S(1)}, bf16[8,128,512]{2,1,0:T(8,128)(2,1)}, u32[]{:S(2)}, u32[]{:S(2)}) collective-permute-start(bf16[8,128,512]{2,1,0:T(8,128)(2,1)S(1)} %get-tuple-element.49), channel_id=1, source_target_pairs={{0,2},{1,3},{2,4},{3,5},{4,6},{5,7},{6,0},{7,1},{8,10},{9,11},{10,... | collective-permute-start | bytes 3145736 | tf_op jit(solution)/shard_map/ppermute | solution.py:43
  224.1 33.4 %collective-permute-start.11 = (bf16[4,64,512]{2,1,0:T(8,128)(2,1)S(1)}, bf16[4,64,512]{2,1,0:T(8,128)(2,1)S(1)}, u32[]{:S(2)}, u32[]{:S(2)}) collective-permute-start(bf16[4,64,512]{2,1,0:T(8,128)(2,1)S(1)} %get-tuple-element.53), channel_id=1, source_target_pairs={{0,64},{1,65},{2,66},{3,67},{4,68},{5,69},{6,70},{7,71},{8,72},{9,... | collective-permute-start | bytes 786440 | tf_op jit(solution)/shard_map/ppermute | solution.py:51
  227.0 32.9 %collective-permute-start.10 = (bf16[4,64,512]{2,1,0:T(8,128)(2,1)S(1)}, bf16[4,64,512]{2,1,0:T(8,128)(2,1)S(1)}, u32[]{:S(2)}, u32[]{:S(2)}) collective-permute-start(bf16[4,64,512]{2,1,0:T(8,128)(2,1)S(1)} %get-tuple-element.54), channel_id=1, source_target_pairs={{0,65},{1,0},{2,67},{3,2},{4,69},{5,4},{6,71},{7,6},{8,73},{9,8},{... | collective-permute-start | bytes 786440 | tf_op jit(solution)/shard_map/ppermute | solution.py:51
  227.0 36.4 %collective-permute-start.9 = (bf16[4,64,512]{2,1,0:T(8,128)(2,1)S(1)}, bf16[4,64,512]{2,1,0:T(8,128)(2,1)S(1)}, u32[]{:S(2)}, u32[]{:S(2)}) collective-permute-start(bf16[4,64,512]{2,1,0:T(8,128)(2,1)S(1)} %get-tuple-element.52), channel_id=1, source_target_pairs={{0,1},{1,64},{2,3},{3,66},{4,5},{5,68},{6,7},{7,70},{8,9},{9,72},{... | collective-permute-start | bytes 786440 | tf_op jit(solution)/shard_map/ppermute | solution.py:51
  263.6 34.9 %collective-permute-start.12 = (bf16[64,512]{1,0:T(8,128)(2,1)S(1)}, bf16[64,512]{1,0:T(8,128)(2,1)S(1)}, u32[]{:S(2)}, u32[]{:S(2)}) collective-permute-start(bf16[64,512]{1,0:T(8,128)(2,1)S(1)} %get-tuple-element.57), channel_id=1, source_target_pairs={{0,16},{1,17},{2,18},{3,19},{4,20},{5,21},{6,22},{7,23},{8,24},{9,... | collective-permute-start | bytes 196616 | tf_op jit(solution)/shard_map/ppermute | solution.py:39
  264.8 33.6 %collective-permute-start.13 = (bf16[64,512]{1,0:T(8,128)(2,1)S(1)}, bf16[64,512]{1,0:T(8,128)(2,1)S(1)}, u32[]{:S(2)}, u32[]{:S(2)}) collective-permute-start(bf16[64,512]{1,0:T(8,128)(2,1)S(1)} %get-tuple-element.56), channel_id=1, source_target_pairs={{0,48},{1,49},{2,50},{3,51},{4,52},{5,53},{6,54},{7,55},{8,56},{9,... | collective-permute-start | bytes 196616 | tf_op jit(solution)/shard_map/ppermute | solution.py:39
  266.6 31.9 %collective-permute-start.14 = (bf16[64,512]{1,0:T(8,128)(2,1)S(1)}, bf16[64,512]{1,0:T(8,128)(2,1)S(1)}, u32[]{:S(2)}, u32[]{:S(2)}) collective-permute-start(bf16[64,512]{1,0:T(8,128)(2,1)S(1)} %get-tuple-element.55), channel_id=1, source_target_pairs={{0,32},{1,33},{2,34},{3,35},{4,36},{5,37},{6,38},{7,39},{8,40},{9,... | collective-permute-start | bytes 196616 | tf_op jit(solution)/shard_map/ppermute | solution.py:39
  279.5 19.7 %copy-start.1 = (bf16[1024,512]{1,0:T(8,128)(2,1)S(1)}, bf16[1024,512]{1,0:T(8,128)(2,1)}, u32[]{:S(2)}) copy-start(bf16[1024,512]{1,0:T(8,128)(2,1)} %param.12) | copy-start | bytes 3145732

commit v5 on v4

--- a/solution.py
+++ b/solution.py
@@ -104,6 +104,7 @@
 
 
 BLOCK = 1024
+PACK = 512
 
 
 def spread_kernel(select_ref, rows_ref, *rest):
@@ -122,13 +123,13 @@
     total = width if beside is None else beside.shape[1]
     return pl.pallas_call(
         spread_kernel,
-        grid=(width // BLOCK,),
+        grid=(width // PACK,),
         in_specs=[
             pl.BlockSpec((slots, 1), lambda j: (0, 0)),
-            pl.BlockSpec((count, BLOCK), lambda j: (0, first // BLOCK + j)),
+            pl.BlockSpec((count, PACK), lambda j: (0, first // PACK + j)),
         ]
         + [pl.BlockSpec(memory_space=pl.ANY)] * len(given),
-        out_specs=pl.BlockSpec((slots, BLOCK), lambda j: (0, j)),
+        out_specs=pl.BlockSpec((slots, PACK), lambda j: (0, j)),
         out_shape=jax.ShapeDtypeStruct((slots, total), jnp.bfloat16),
         input_output_aliases={2: 0} if given else {},
         scratch_shapes=[pltpu.VMEM((slots, count), jnp.bfloat16)],

time: 300 us -> 301 us (level)
  no operation moved by 1% of the time
where the time goes in v5:
time: 301 us; the launch traced here: 300 us
  waiting for transfers between devices  139 us (46%)
  Pallas kernels  64.2 us (21%)
  starting transfers between devices  47.7 us (16%)
  local copies, waits for them, and re-layouts  18.8 us (6%)
  other arithmetic  18.3 us (6%)
  matrix products  11 us (4%)
    ppermute x6, waiting for transfers between devices, along_y(): lax.ppermute(v, AXES, perm(lambda zh, x, c, y, zl: (zh, x, c, y + n, zl)))  64.7 us
    ppermute x3, waiting for transfers between devices, along_z(): return lax.ppermute(v, AXES, perm(step))  34.9 us
    all_to_all x2, waiting for transfers between devices, exchange(): lax.all_to_all(blocks, 'dp', split_axis=0, concat_axis=0, tiled=True)  32 us
    pallas_call x2, Pallas kernels, spread_rows(): pl.pallas_call(spread_kernel, grid=(width // PACK,), in_specs=[pl.BlockSp...  21.1 us
    pallas_call x1, Pallas kernels, last_pass(): pl.pallas_call(functools.partial(last_pass_kernel, early=early, late=late...  19 us
    ppermute x3, starting transfers between devices, along_x(): lax.ppermute(v, AXES, perm(lambda zh, x, c, y, zl: (zh, x + n, c, y, zl)))  15.9 us
    all_to_all x2, starting transfers between devices, exchange(): lax.all_to_all(blocks, 'dp', split_axis=0, concat_axis=0, tiled=True)  14.9 us
    pallas_call x1, Pallas kernels, scaled_delta(): pl.pallas_call(delta_kernel, grid_spec=pltpu.PrefetchScalarGridSpec(num_s...  11.4 us
  transfers between devices with their start and end apart: 17, of which 9 were waited for; matrix products, arithmetic and copies ran while one was open for 15% of the time, Pallas kernels for 21%

profile of v5, /device:TPU:1, one launch (start us, length us, event | category | flops | bytes accessed | tf_op | source)
XLA Modules:
  0.0 299.9 jit_solution(17107471749812022308)
XLA Ops:
  1.9 2.5 collective-permute-start
  11.6 3.3 %rope_and_spread.1 = (bf16[512,512]{1,0:T(8,128)(2,1)}, bf16[1024,3584]{1,0:T(8,128)(2,1)}) custom-call(s32[1024,1]{1,0:T(8,128)} %select_n.242.select_ref, f32[512,128]{1,0:T(8,128)} %get-tuple-element.60.cos_ref, f32[512,128]{1,0:T(8,128)} %get-tuple-element.59.sin_ref, bf16[512,512]{1,0:T(8,128)(2,1)} %rotated_ref.1), custom_call_target="tpu_custom_call" | custom-call | flops 536870912 | bytes 4194304 | tf_op jit(solution)/shard_map/rope_and_spread/pallas_call | solution.py:91
  14.9 8.2 %spread_rows.2 = bf16[1024,3584]{1,0:T(8,128)(2,1)} custom-call(s32[1024,1]{1,0:T(8,128)} %select_n.243.select_ref, bf16[512,8192]{1,0:T(8,128)(2,1)} %rows_ref.3, bf16[1024,3584]{1,0:T(8,128)(2,1)} %get-tuple-element.22.rest_0_), custom_call_target="tpu_custom_call", output_to_operand_aliasing={{}: (2, {})} | custom-call | flops 3221225472 | bytes 9437184 | tf_op jit(solution)/shard_map/spread_rows/pallas_call | solution.py:124
  23.1 8.3 %all-to-all-start = ((bf16[16,64,3584]{2,1,0:T(8,128)(2,1)}), bf16[16,64,3584]{2,1,0:T(8,128)(2,1)}, u32[]{:S(2)}, u32[]{:S(2)}) async-start(bf16[16,64,3584]{2,1,0:T(8,128)(2,1)} %bitcast.67), calls=%async_computation | async-start | bytes 14680064 | tf_op jit(solution)/shard_map/all_to_all | solution.py:378
  37.5 21.2 %collective-permute-done.1 = bf16[2,512,512]{2,1,0:T(8,128)(2,1)} collective-permute-done((bf16[2,512,512]{2,1,0:T(8,128)(2,1)}, bf16[2,512,512]{2,1,0:T(8,128)(2,1)}, u32[]{:S(2)}, u32[]{:S(2)}) %collective-permute-start.1) | collective-permute-done | bytes 1048608 | tf_op jit(solution)/shard_map/ppermute | solution.py:43
  61.4 20.9 %collective-permute-done.3 = bf16[2,512,512]{2,1,0:T(8,128)(2,1)} collective-permute-done((bf16[2,512,512]{2,1,0:T(8,128)(2,1)}, bf16[2,512,512]{2,1,0:T(8,128)(2,1)}, u32[]{:S(2)}, u32[]{:S(2)}) %collective-permute-start.3) | collective-permute-done | bytes 1048608 | tf_op jit(solution)/shard_map/ppermute | solution.py:43
  84.7 12.9 %spread_rows.3 = bf16[1024,5120]{1,0:T(8,128)(2,1)} custom-call(s32[1024,1]{1,0:T(8,128)} %select_n.243.select_ref, bf16[512,8192]{1,0:T(8,128)(2,1)} %rows_ref.3), custom_call_target="tpu_custom_call" | custom-call | flops 5368709120 | bytes 15728640 | tf_op jit(solution)/shard_map/spread_rows/pallas_call | solution.py:124
  97.7 32.0 %all-to-all-done = bf16[16,64,3584]{2,1,0:T(8,128)(2,1)} async-done(((bf16[16,64,3584]{2,1,0:T(8,128)(2,1)}), bf16[16,64,3584]{2,1,0:T(8,128)(2,1)}, u32[]{:S(2)}, u32[]{:S(2)}) %all-to-all-start) | async-done | bytes 7340064 | tf_op jit(solution)/shard_map/all_to_all | solution.py:378
  129.7 6.6 %all-to-all-start.1 = ((bf16[16,64,5120]{2,1,0:T(8,128)(2,1)}), bf16[16,64,5120]{2,1,0:T(8,128)(2,1)}, u32[]{:S(2)}, u32[]{:S(2)}) async-start(bf16[16,64,5120]{2,1,0:T(8,128)(2,1)} %bitcast.72), calls=%async_computation.1 | async-start | bytes 20971520 | tf_op jit(solution)/shard_map/all_to_all | solution.py:378
  136.4 5.1 %fusion = f32[512]{0:T(512)S(1)} fusion(bf16[512,8192]{1,0:T(8,128)(2,1)} %rows_ref.3), kind=kLoop, calls=%fused_computation.2 | loop fusion | flops 12582400 | bytes 8390656 | tf_op jit(solution)/shard_map/reduce_sum | solution.py:417
  141.5 11.0 %multiply_convert_fusion = bf16[8192,512]{1,0:T(8,128)(2,1)} fusion(bf16[512,8192]{1,0:T(8,128)(2,1)} %rows_ref.3, f32[8192]{0:T(1024)S(1)} %convert_element_type.87, f32[512]{0:T(512)S(1)} %add_rsqrt_fusion, bf16[1024,3584]{1,0:T(8,128)(2,1)} %bitcast.7.arrived_ref, s32[1024]{0:T(1024)S(1)} %select_n.217), kind=kOutput, calls=%fused_computation.5 | convolution fusion | flops 4857790464 | bytes 17864704 | tf_op jit(solution)/shard_map/dot_general | solution.py:421
  152.6 4.4 %dynamic-slice_bitcast_fusion = bf16[8,512,512]{2,1,0:T(8,128)(2,1)} fusion(bf16[8,2,512,512]{3,2,1,0:T(8,128)(2,1)} %bitcast.73, s32[]{:T(128)S(6)} %select_n.218), kind=kLoop, calls=%fused_computation.10 | loop fusion | bytes 8388612 | tf_op jit(solution)/shard_map/jit(dynamic_index_in_dim)/squeeze | solution.py:59
  157.2 7.4 %collective-permute-done.5 = bf16[8,512,512]{2,1,0:T(8,128)(2,1)} collective-permute-done((bf16[8,512,512]{2,1,0:T(8,128)(2,1)}, bf16[8,512,512]{2,1,0:T(8,128)(2,1)}, u32[]{:S(2)}, u32[]{:S(2)}) %collective-permute-start.5) | collective-permute-done | bytes 4194336 | tf_op jit(solution)/shard_map/ppermute | solution.py:35
  164.5 4.7 %fusion.4 = bf16[8,512,512]{2,1,0:T(8,128)(2,1)S(1)} fusion(bf16[8,512,512]{2,1,0:T(8,128)(2,1)} %collective-permute-done.5, bf16[8,2,512,512]{3,2,1,0:T(8,128)(2,1)} %bitcast.74, s32[]{:T(128)S(6)} %select_n.203), kind=kLoop, calls=%fused_computation.7 | loop fusion | flops 8388608 | bytes 12582916 | tf_op jit(solution)/shard_map/convert_element_type | solution.py:427
  172.8 2.9 collective-permute-start.8
  178.1 11.4 %scaled_delta.1.scaled_ref = bf16[512,8192]{1,0:T(8,128)(2,1)} custom-call(s32[1]{0:T(128)} %bitcast.17.core_ref, bf16[512,512]{1,0:T(8,128)(2,1)} %get-tuple-element.26.key_ref, bf16[8,512,512]{2,1,0:T(8,128)(2,1)} %bitcast.69, bf16[8,512,512]{2,1,0:T(8,128)(2,1)} %collective-permute-done.4.other_ref, f32[1,8192]{1,0:T(1,128)} %bitcast.80), custom_call_target="tpu_custom_call" | custom-call | flops 4294967296 | bytes 16777216 | tf_op jit(solution)/shard_map/scaled_delta/pallas_call | solution.py:166
  190.3 9.4 %first_pass.1 = (bf16[512,3072]{1,0:T(8,128)(2,1)}, f32[512,128]{1,0:T(8,128)}, f32[512,128]{1,0:T(8,128)}) custom-call(s32[512,1]{1,0:T(8,128)} %iota_add_fusion.select_ref, bf16[1024,3584]{1,0:T(8,128)(2,1)} %bitcast.7.arrived_ref, bf16[512,8192]{1,0:T(8,128)(2,1)} %scaled_delta.1.scaled_ref, f32[512,128]{1,0:T(8,128)} %broadcast_2_square_in_inner_in.2.square_in.inner_in, ...), custom_call_target="tpu_custom_call" | custom-call | flops 3221225472 | bytes 15728640 | tf_op jit(solution)/shard_map/first_pass/pallas_call | solution.py:226
  199.6 22.5 %collective-permute-done.7 = bf16[8,128,512]{2,1,0:T(8,128)(2,1)} collective-permute-done((bf16[8,128,512]{2,1,0:T(8,128)(2,1)}, bf16[8,128,512]{2,1,0:T(8,128)(2,1)}, u32[]{:S(2)}, u32[]{:S(2)}) %collective-permute-start.7) | collective-permute-done | bytes 1048608 | tf_op jit(solution)/shard_map/ppermute | solution.py:43
  224.8 3.0 collective-permute-start.11
  229.2 29.0 %collective-permute-done.11 = bf16[4,64,512]{2,1,0:T(8,128)(2,1)S(1)} collective-permute-done((bf16[4,64,512]{2,1,0:T(8,128)(2,1)S(1)}, bf16[4,64,512]{2,1,0:T(8,128)(2,1)S(1)}, u32[]{:S(2)}, u32[]{:S(2)}) %collective-permute-start.11) | collective-permute-done | bytes 262176 | tf_op jit(solution)/shard_map/ppermute | solution.py:51
  258.2 2.5 collective-permute-done.10
  260.7 3.4 %collective-permute-done.9 = bf16[4,64,512]{2,1,0:T(8,128)(2,1)S(1)} collective-permute-done((bf16[4,64,512]{2,1,0:T(8,128)(2,1)S(1)}, bf16[4,64,512]{2,1,0:T(8,128)(2,1)S(1)}, u32[]{:S(2)}, u32[]{:S(2)}) %collective-permute-start.9) | collective-permute-done | bytes 262176 | tf_op jit(solution)/shard_map/ppermute | solution.py:51
  267.4 12.9 %collective-permute-start.14 = (bf16[64,512]{1,0:T(8,128)(2,1)S(1)}, bf16[64,512]{1,0:T(8,128)(2,1)S(1)}, u32[]{:S(2)}, u32[]{:S(2)}) collective-permute-start(bf16[64,512]{1,0:T(8,128)(2,1)S(1)} %get-tuple-element.55), channel_id=1, source_target_pairs={{0,32},{1,33},{2,34},{3,35},{4,36},{5,37},{6,38},{7,39},{8,40},{9,... | collective-permute-start | bytes 196616 | tf_op jit(solution)/shard_map/ppermute | solution.py:39
  280.3 19.0 %last_pass.1 = bf16[512,8192]{1,0:T(8,128)(2,1)} custom-call(s32[512,1]{1,0:T(8,128)} %iota_add_fusion.select_ref, bf16[1024,5120]{1,0:T(8,128)(2,1)} %bitcast.16.arrived_ref, bf16[512,8192]{1,0:T(8,128)(2,1)} %scaled_delta.1.scaled_ref, bf16[512,3072]{1,0:T(8,128)(2,1)} %get-tuple-element.30.packed_ref, f32[512,128]{1,0:T(8,128)} %get-tuple-element.34.square_in, ...), custom_call_target="tpu_custom_call" | custom-call | flops 5368709120 | bytes 25165824 | tf_op jit(solution)/shard_map/last_pass/pallas_call | solution.py:289
  (68 shorter events, 34.5 us)
Async XLA Ops:
  0.6 1.2 copy-start
  1.9 21.2 %collective-permute-start = (bf16[512,512]{1,0:T(8,128)(2,1)S(1)}, bf16[512,512]{1,0:T(8,128)(2,1)S(1)}, u32[]{:S(2)}, u32[]{:S(2)}) collective-permute-start(bf16[512,512]{1,0:T(8,128)(2,1)S(1)} %fusion.26), channel_id=1, source_target_pairs={{0,1},{1,0},{2,3},{3,2},{4,5},{5,4},{6,7},{7,6},{8,9},{9,8},{10,11... | collective-permute-start | bytes 1572872 | tf_op jit(solution)/shard_map/ppermute | solution.py:55
  23.1 106.7 %all-to-all-start = ((bf16[16,64,3584]{2,1,0:T(8,128)(2,1)}), bf16[16,64,3584]{2,1,0:T(8,128)(2,1)}, u32[]{:S(2)}, u32[]{:S(2)}) async-start(bf16[16,64,3584]{2,1,0:T(8,128)(2,1)} %bitcast.67), calls=%async_computation | async-start | bytes 14680064 | tf_op jit(solution)/shard_map/all_to_all | solution.py:378
  32.5 26.2 %collective-permute-start.1 = (bf16[2,512,512]{2,1,0:T(8,128)(2,1)}, bf16[2,512,512]{2,1,0:T(8,128)(2,1)}, u32[]{:S(2)}, u32[]{:S(2)}) collective-permute-start(bf16[2,512,512]{2,1,0:T(8,128)(2,1)} %maximum_select_fusion.1), channel_id=1, source_target_pairs={{0,2},{1,3},{2,4},{3,5},{4,6},{5,7},{6,0},{7,1},{8,10},{9,11},{10,... | collective-permute-start | bytes 3145736 | tf_op jit(solution)/shard_map/ppermute | solution.py:43
  33.8 26.3 %collective-permute-start.2 = (bf16[2,512,512]{2,1,0:T(8,128)(2,1)}, bf16[2,512,512]{2,1,0:T(8,128)(2,1)}, u32[]{:S(2)}, u32[]{:S(2)}) collective-permute-start(bf16[2,512,512]{2,1,0:T(8,128)(2,1)} %maximum_select_fusion.1), channel_id=1, source_target_pairs={{0,6},{1,7},{2,0},{3,1},{4,2},{5,3},{6,4},{7,5},{8,14},{9,15},{10,... | collective-permute-start | bytes 3145736 | tf_op jit(solution)/shard_map/ppermute | solution.py:43
  35.3 47.1 %collective-permute-start.3 = (bf16[2,512,512]{2,1,0:T(8,128)(2,1)}, bf16[2,512,512]{2,1,0:T(8,128)(2,1)}, u32[]{:S(2)}, u32[]{:S(2)}) collective-permute-start(bf16[2,512,512]{2,1,0:T(8,128)(2,1)} %maximum_select_fusion.1), channel_id=1, source_target_pairs={{0,4},{1,5},{2,6},{3,7},{4,0},{5,1},{6,2},{7,3},{8,12},{9,13},{10,... | collective-permute-start | bytes 3145736 | tf_op jit(solution)/shard_map/ppermute | solution.py:43
  83.7 14.0 %copy-start.2 = (bf16[4,2,512,512]{3,2,1,0:T(8,128)(2,1)}, bf16[4,2,512,512]{3,2,1,0:T(8,128)(2,1)S(1)}, u32[]{:S(2)}) copy-start(bf16[4,2,512,512]{3,2,1,0:T(8,128)(2,1)S(1)} %bitcast_dynamic-update-slice_fusion) | copy-start | bytes 12582916
  83.7 14.0 %collective-permute-start.4 = (bf16[8,512,512]{2,1,0:T(8,128)(2,1)S(1)}, bf16[8,512,512]{2,1,0:T(8,128)(2,1)}, u32[]{:S(2)}, u32[]{:S(2)}) collective-permute-start(bf16[8,512,512]{2,1,0:T(8,128)(2,1)S(1)} %bitcast.68), channel_id=1, source_target_pairs={{0,8},{1,9},{2,10},{3,11},{4,12},{5,13},{6,14},{7,15},{8,0},{9,1},... | collective-permute-start | bytes 12582920 | tf_op jit(solution)/shard_map/ppermute | solution.py:35
  129.7 6.7 %copy-start.5 = (bf16[8192]{0:T(1024)(128)(2,1)S(1)}, bf16[8192]{0:T(1024)(128)(2,1)}, u32[]{:S(2)}) copy-start(bf16[8192]{0:T(1024)(128)(2,1)} %param.11) | copy-start | bytes 49156
  129.7 150.5 %all-to-all-start.1 = ((bf16[16,64,5120]{2,1,0:T(8,128)(2,1)}), bf16[16,64,5120]{2,1,0:T(8,128)(2,1)}, u32[]{:S(2)}, u32[]{:S(2)}) async-start(bf16[16,64,5120]{2,1,0:T(8,128)(2,1)} %bitcast.72), calls=%async_computation.1 | async-start | bytes 20971520 | tf_op jit(solution)/shard_map/all_to_all | solution.py:378
  136.4 5.1 %copy-start.4 = (f32[8192]{0:T(1024)}, f32[8192]{0:T(1024)S(1)}, u32[]{:S(2)}) copy-start(f32[8192]{0:T(1024)S(1)} %convert_element_type.87) | copy-start | bytes 98308
  157.0 7.5 %collective-permute-start.5 = (bf16[8,512,512]{2,1,0:T(8,128)(2,1)}, bf16[8,512,512]{2,1,0:T(8,128)(2,1)}, u32[]{:S(2)}, u32[]{:S(2)}) collective-permute-start(bf16[8,512,512]{2,1,0:T(8,128)(2,1)} %dynamic-slice_bitcast_fusion), channel_id=1, source_target_pairs={{0,8},{1,9},{2,10},{3,11},{4,12},{5,13},{6,14},{7,15},{8,0},{9,1},... | collective-permute-start | bytes 12582920 | tf_op jit(solution)/shard_map/ppermute | solution.py:35
  169.2 2.0 copy-start.3
  172.8 26.8 %collective-permute-start.8 = (bf16[8,128,512]{2,1,0:T(8,128)(2,1)}, bf16[8,128,512]{2,1,0:T(8,128)(2,1)S(1)}, u32[]{:S(2)}, u32[]{:S(2)}) collective-permute-start(bf16[8,128,512]{2,1,0:T(8,128)(2,1)} %get-tuple-element.50), channel_id=1, source_target_pairs={{0,4},{1,5},{2,6},{3,7},{4,0},{5,1},{6,2},{7,3},{8,12},{9,13},{10,... | collective-permute-start | bytes 3145736 | tf_op jit(solution)/shard_map/ppermute | solution.py:43
  175.7 46.4 %collective-permute-start.7 = (bf16[8,128,512]{2,1,0:T(8,128)(2,1)}, bf16[8,128,512]{2,1,0:T(8,128)(2,1)}, u32[]{:S(2)}, u32[]{:S(2)}) collective-permute-start(bf16[8,128,512]{2,1,0:T(8,128)(2,1)} %get-tuple-element.51), channel_id=1, source_target_pairs={{0,6},{1,7},{2,0},{3,1},{4,2},{5,3},{6,4},{7,5},{8,14},{9,15},{10,... | collective-permute-start | bytes 3145736 | tf_op jit(solution)/shard_map/ppermute | solution.py:43
  176.5 45.7 %collective-permute-start.6 = (bf16[8,128,512]{2,1,0:T(8,128)(2,1)S(1)}, bf16[8,128,512]{2,1,0:T(8,128)(2,1)}, u32[]{:S(2)}, u32[]{:S(2)}) collective-permute-start(bf16[8,128,512]{2,1,0:T(8,128)(2,1)S(1)} %get-tuple-element.49), channel_id=1, source_target_pairs={{0,2},{1,3},{2,4},{3,5},{4,6},{5,7},{6,0},{7,1},{8,10},{9,11},{10,... | collective-permute-start | bytes 3145736 | tf_op jit(solution)/shard_map/ppermute | solution.py:43
  224.8 33.4 %collective-permute-start.11 = (bf16[4,64,512]{2,1,0:T(8,128)(2,1)S(1)}, bf16[4,64,512]{2,1,0:T(8,128)(2,1)S(1)}, u32[]{:S(2)}, u32[]{:S(2)}) collective-permute-start(bf16[4,64,512]{2,1,0:T(8,128)(2,1)S(1)} %get-tuple-element.53), channel_id=1, source_target_pairs={{0,64},{1,65},{2,66},{3,67},{4,68},{5,69},{6,70},{7,71},{8,72},{9,... | collective-permute-start | bytes 786440 | tf_op jit(solution)/shard_map/ppermute | solution.py:51
  227.8 32.9 %collective-permute-start.10 = (bf16[4,64,512]{2,1,0:T(8,128)(2,1)S(1)}, bf16[4,64,512]{2,1,0:T(8,128)(2,1)S(1)}, u32[]{:S(2)}, u32[]{:S(2)}) collective-permute-start(bf16[4,64,512]{2,1,0:T(8,128)(2,1)S(1)} %get-tuple-element.54), channel_id=1, source_target_pairs={{0,65},{1,0},{2,67},{3,2},{4,69},{5,4},{6,71},{7,6},{8,73},{9,8},{... | collective-permute-start | bytes 786440 | tf_op jit(solution)/shard_map/ppermute | solution.py:51
  227.8 36.4 %collective-permute-start.9 = (bf16[4,64,512]{2,1,0:T(8,128)(2,1)S(1)}, bf16[4,64,512]{2,1,0:T(8,128)(2,1)S(1)}, u32[]{:S(2)}, u32[]{:S(2)}) collective-permute-start(bf16[4,64,512]{2,1,0:T(8,128)(2,1)S(1)} %get-tuple-element.52), channel_id=1, source_target_pairs={{0,1},{1,64},{2,3},{3,66},{4,5},{5,68},{6,7},{7,70},{8,9},{9,72},{... | collective-permute-start | bytes 786440 | tf_op jit(solution)/shard_map/ppermute | solution.py:51
  264.3 34.9 %collective-permute-start.12 = (bf16[64,512]{1,0:T(8,128)(2,1)S(1)}, bf16[64,512]{1,0:T(8,128)(2,1)S(1)}, u32[]{:S(2)}, u32[]{:S(2)}) collective-permute-start(bf16[64,512]{1,0:T(8,128)(2,1)S(1)} %get-tuple-element.57), channel_id=1, source_target_pairs={{0,16},{1,17},{2,18},{3,19},{4,20},{5,21},{6,22},{7,23},{8,24},{9,... | collective-permute-start | bytes 196616 | tf_op jit(solution)/shard_map/ppermute | solution.py:39
  265.6 33.6 %collective-permute-start.13 = (bf16[64,512]{1,0:T(8,128)(2,1)S(1)}, bf16[64,512]{1,0:T(8,128)(2,1)S(1)}, u32[]{:S(2)}, u32[]{:S(2)}) collective-permute-start(bf16[64,512]{1,0:T(8,128)(2,1)S(1)} %get-tuple-element.56), channel_id=1, source_target_pairs={{0,48},{1,49},{2,50},{3,51},{4,52},{5,53},{6,54},{7,55},{8,56},{9,... | collective-permute-start | bytes 196616 | tf_op jit(solution)/shard_map/ppermute | solution.py:39
  267.4 31.9 %collective-permute-start.14 = (bf16[64,512]{1,0:T(8,128)(2,1)S(1)}, bf16[64,512]{1,0:T(8,128)(2,1)S(1)}, u32[]{:S(2)}, u32[]{:S(2)}) collective-permute-start(bf16[64,512]{1,0:T(8,128)(2,1)S(1)} %get-tuple-element.55), channel_id=1, source_target_pairs={{0,32},{1,33},{2,34},{3,35},{4,36},{5,37},{6,38},{7,39},{8,40},{9,... | collective-permute-start | bytes 196616 | tf_op jit(solution)/shard_map/ppermute | solution.py:39
  280.3 19.7 %copy-start.1 = (bf16[1024,512]{1,0:T(8,128)(2,1)S(1)}, bf16[1024,512]{1,0:T(8,128)(2,1)}, u32[]{:S(2)}) copy-start(bf16[1024,512]{1,0:T(8,128)(2,1)} %param.12) | copy-start | bytes 3145732
